TPU v7x, 32 devices: a whole 2x2x4 slice. The times are simulated.
32 devices in a mesh: set: 8 (over y, x, core), path: 4 (over z).
Axes of the slice: x: 2, y: 2, z: 4, core: 2. Of those that a mesh axis runs over, the one named last changes fastest.
Arguments:
- start_state: float32 [512, 2048], P(('path', 'set')), may hold values from -6 to 6
- shocks: bfloat16 [2, 512, 2048], P(None, ('path', 'set')), may hold values from -6 to 6
- loading: bfloat16 [2048, 2048], replicated, may hold values from -0.125 to 0.125
- decay: float32 [2048], replicated, may hold values from 0.5 to 1
- factor_lists: int32 [1024, 64], P('set'), may hold values from 0 to 2047, all different within a row
- delta: bfloat16 [1024, 64], P('set'), may hold values from -0.75 to 0.75
- gamma: bfloat16 [1024, 64, 64], P('set'), may hold values from -0.09375 to 0.09375
- currency: int32 [1024], P('set'), may hold values from 0 to 15
- owner: int32 [1024], P('set'), may hold values from 0 to 63
Outputs:
- exposure: float32 [2, 64, 512], P(None, 'set', 'path')
- end_state: float32 [512, 2048], P(('path', 'set'))
Inputs may be any that keep to these rules, and one draw needn't show every extreme that they name: `factor_lists`: the 64 factors of one netting set are different.
All inputs are finite; a program needn't handle non-finite values.
Results may differ from a plain program's by a relative error of at most 0.004.
Values may be sent and summed in bfloat16 or wider, within the bound.
A program may use at most 64 MiB of HBM per device.

v0:
```python
import math

import jax
import jax.numpy as jnp
from jax import lax
from jax.sharding import PartitionSpec as P

NB = 16
STEPS = 2
PDEV = 16
CP_DEV = 8


def value_block(slab, lists_b, delta_b, gamma_b, cur_b):
    rows = slab.shape[0]
    count = lists_b.shape[0]
    picked = jnp.take(slab, lists_b.reshape(-1), axis=1).reshape(rows, count, lists_b.shape[1])
    curved = jnp.einsum("psk,skl->psl", picked, gamma_b, preferred_element_type=jnp.float32)
    linear = delta_b.astype(jnp.float32)[None] + 0.5 * curved
    local = jnp.sum(picked.astype(jnp.float32) * linear, axis=2)
    rates = jnp.exp(0.2 * jnp.take(slab, cur_b, axis=1).astype(jnp.float32))
    return (local * rates).T


def revalue(slab, lists, delta, gamma, cur):
    total = lists.shape[0]
    width = math.gcd(16, total)
    blocks = total // width
    depth = lists.shape[1]
    stacked = lax.map(
        lambda a: value_block(slab, a[0], a[1], a[2], a[3]),
        (
            lists.reshape(blocks, width, depth),
            delta.reshape(blocks, width, depth),
            gamma.reshape(blocks, width, depth, depth),
            cur.reshape(blocks, width),
        ),
    )
    return stacked.reshape(total, slab.shape[0])


def regress(gram, moments, total):
    size = gram.shape[0]
    chol = jnp.linalg.cholesky(gram / total + 0.001 * jnp.eye(size, dtype=jnp.float32))
    middle = lax.linalg.triangular_solve(chol, moments / total, left_side=True, lower=True)
    return lax.linalg.triangular_solve(chol, middle, left_side=True, lower=True, transpose_a=True)


def per_device(start_state, shocks, loading, decay, factor_lists, delta, gamma, currency, owner):
    high = lax.Precision.HIGHEST
    groups = lax.axis_size("set")
    member = lax.axis_index("set")
    total_paths = PDEV * groups * lax.axis_size("path")
    set_count = factor_lists.shape[0]
    onehot = (owner[None, :] == jnp.arange(CP_DEV * groups, dtype=jnp.int32)[:, None]).astype(
        jnp.float32
    )

    def evaluate(piece):
        values = revalue(piece, factor_lists, delta, gamma, currency)
        return jnp.concatenate([values, piece[:, :NB].astype(jnp.float32).T], axis=0)

    def evaluate_steps(piece):
        return jnp.stack([evaluate(piece[step]) for step in range(STEPS)])

    state = start_state
    slabs = []
    evaluated = []
    for step in range(STEPS):
        state = decay[None, :] * state + jnp.dot(
            shocks[step], loading, preferred_element_type=jnp.float32
        )
        slab = state.astype(jnp.bfloat16)
        slabs.append(slab)
    joined = evaluate_steps(lax.all_gather(jnp.stack(slabs), "set", axis=1, tiled=True))
    evaluated = [joined[step] for step in range(STEPS)]
    results = []
    for step in range(STEPS):
        values = evaluated[step][:set_count]
        factors = evaluated[step][set_count:]
        summed = lax.psum(jnp.dot(onehot, values, precision=high), "set")
        netted = lax.dynamic_slice_in_dim(summed, member * CP_DEV, CP_DEV, 0)
        ones = jnp.ones((1, values.shape[1]), jnp.float32)
        basis = jnp.concatenate([ones, factors], axis=0)
        gram, moments = lax.psum(
            (jnp.dot(basis, basis.T, precision=high), jnp.dot(basis, netted.T, precision=high)),
            "path",
        )
        coef = regress(gram, moments, total_paths)
        fitted = jnp.dot(coef.T, basis, precision=high)
        results.append(jnp.maximum(netted - 0.9 * fitted, 0.0))
    return (jnp.stack(results), state)


def solution(mesh):
    return jax.shard_map(
        per_device,
        mesh=mesh,
        in_specs=(
            P(("path", "set"), None),
            P(None, ("path", "set"), None),
            P(),
            P(),
            P("set", None),
            P("set", None),
            P("set", None, None),
            P("set"),
            P("set"),
        ),
        out_specs=(P(None, "set", "path"), P(("path", "set"), None)),
        check_vma=False,
    )
```

profile of v0, /device:TPU:0, one launch (start us, length us, event | category | flops | bytes accessed | tf_op | source)
XLA Modules:
  0.0 225.1 jit_solution(3285633796988835652)
XLA Ops:
  7.2 4.7 %convolution_add_fusion.1 = f32[16,2048]{1,0:T(8,128)S(1)} fusion(bf16[2048,2048]{1,0:T(8,128)(2,1)} %param.24, f32[16,2048]{1,0:T(8,128)} %param.22, bf16[2,16,2048]{2,1,0:T(8,128)(2,1)} %param.23, f32[2048]{0:T(1024)} %param.25), kind=kOutput, calls=%fused_computation.45 | convolution fusion | flops 134283264 | bytes 8724480 | tf_op jit(solution)/shard_map/dot_general | solution.py:70
  12.0 1.1 copy-done
  13.1 1.2 convolution_add_fusion
  15.3 4.5 %copy.13 = bf16[128,64,64]{1,2,0:T(8,128)(2,1)} copy(bf16[128,64,64]{0,2,1:T(8,128)(2,1)S(1)} %copy-done.1) | data formatting | bytes 2097152 | tf_op args[6]
  19.9 21.5 %all-gather.2.cloned.1.call-done = bf16[2,128,2048]{2,1,0:T(8,128)(2,1)} async-done(((bf16[2,16,2048]{2,1,0:T(8,128)(2,1)}), bf16[2,128,2048]{2,1,0:T(8,128)(2,1)}) %all-gather.2.cloned.1.call-update) | async-done | bytes 1048592 | tf_op jit(solution)/shard_map/all_gather | solution.py:75
  41.4 1.3 slice_bitcast_fusion.1
  43.5 43.6 %while.21 = (s32[]{:T(128)}, f32[8,16,128]{2,1,0:T(8,128)S(1)}, s32[8,16,64]{2,1,0:T(8,128)S(1)}, bf16[128,2048]{0,1:T(8,128)(2,1)S(1)}, bf16[8,16,64]{2,1,0:T(8...) while((s32[]{:T(128)}, f32[8,16,128]{2,1,0:T(8,128)S(1)}, ...), condition=%wide.region_10.16_spmd, body=%wide.region_8.15_spmd.sunk | while | flops 17582176 | bytes 1926017 | solution.py:30
  43.6 3.2 %gather_fusion.2 = bf16[1024,128]{1,0:T(8,128)(2,1)S(1)} fusion(bf16[128,2048]{0,1:T(8,128)(2,1)S(1)} %get-tuple-element.252, s32[1024]{0:T(1024)S(1)} %fusion.94), kind=kCustom, calls=%fused_computation.2.clone.clone.1 | custom fusion | bytes 528384 | tf_op jit(solution)/shard_map/while/body/eval_jaxpr/jit(_take)/gather | solution.py:17
  47.1 1.2 fusion.95
  49.1 3.2 %gather_fusion.2 = bf16[1024,128]{1,0:T(8,128)(2,1)S(1)} fusion(bf16[128,2048]{0,1:T(8,128)(2,1)S(1)} %get-tuple-element.252, s32[1024]{0:T(1024)S(1)} %fusion.94), kind=kCustom, calls=%fused_computation.2.clone.clone.1 | custom fusion | bytes 528384 | tf_op jit(solution)/shard_map/while/body/eval_jaxpr/jit(_take)/gather | solution.py:17
  52.5 1.2 fusion.95
  54.5 3.2 %gather_fusion.2 = bf16[1024,128]{1,0:T(8,128)(2,1)S(1)} fusion(bf16[128,2048]{0,1:T(8,128)(2,1)S(1)} %get-tuple-element.252, s32[1024]{0:T(1024)S(1)} %fusion.94), kind=kCustom, calls=%fused_computation.2.clone.clone.1 | custom fusion | bytes 528384 | tf_op jit(solution)/shard_map/while/body/eval_jaxpr/jit(_take)/gather | solution.py:17
  58.0 1.2 fusion.95
  60.0 3.2 %gather_fusion.2 = bf16[1024,128]{1,0:T(8,128)(2,1)S(1)} fusion(bf16[128,2048]{0,1:T(8,128)(2,1)S(1)} %get-tuple-element.252, s32[1024]{0:T(1024)S(1)} %fusion.94), kind=kCustom, calls=%fused_computation.2.clone.clone.1 | custom fusion | bytes 528384 | tf_op jit(solution)/shard_map/while/body/eval_jaxpr/jit(_take)/gather | solution.py:17
  63.4 1.2 fusion.95
  65.4 3.2 %gather_fusion.2 = bf16[1024,128]{1,0:T(8,128)(2,1)S(1)} fusion(bf16[128,2048]{0,1:T(8,128)(2,1)S(1)} %get-tuple-element.252, s32[1024]{0:T(1024)S(1)} %fusion.94), kind=kCustom, calls=%fused_computation.2.clone.clone.1 | custom fusion | bytes 528384 | tf_op jit(solution)/shard_map/while/body/eval_jaxpr/jit(_take)/gather | solution.py:17
  68.9 1.2 fusion.95
  70.8 3.2 %gather_fusion.2 = bf16[1024,128]{1,0:T(8,128)(2,1)S(1)} fusion(bf16[128,2048]{0,1:T(8,128)(2,1)S(1)} %get-tuple-element.252, s32[1024]{0:T(1024)S(1)} %fusion.94), kind=kCustom, calls=%fused_computation.2.clone.clone.1 | custom fusion | bytes 528384 | tf_op jit(solution)/shard_map/while/body/eval_jaxpr/jit(_take)/gather | solution.py:17
  74.3 1.2 fusion.95
  76.3 3.2 %gather_fusion.2 = bf16[1024,128]{1,0:T(8,128)(2,1)S(1)} fusion(bf16[128,2048]{0,1:T(8,128)(2,1)S(1)} %get-tuple-element.252, s32[1024]{0:T(1024)S(1)} %fusion.94), kind=kCustom, calls=%fused_computation.2.clone.clone.1 | custom fusion | bytes 528384 | tf_op jit(solution)/shard_map/while/body/eval_jaxpr/jit(_take)/gather | solution.py:17
  79.7 1.2 fusion.95
  81.7 3.2 %gather_fusion.2 = bf16[1024,128]{1,0:T(8,128)(2,1)S(1)} fusion(bf16[128,2048]{0,1:T(8,128)(2,1)S(1)} %get-tuple-element.252, s32[1024]{0:T(1024)S(1)} %fusion.94), kind=kCustom, calls=%fused_computation.2.clone.clone.1 | custom fusion | bytes 528384 | tf_op jit(solution)/shard_map/while/body/eval_jaxpr/jit(_take)/gather | solution.py:17
  85.2 1.2 fusion.95
  87.1 43.6 %while.20 = (s32[]{:T(128)}, f32[8,16,128]{2,1,0:T(8,128)S(1)}, s32[8,16,64]{2,1,0:T(8,128)S(1)}, bf16[128,2048]{0,1:T(8,128)(2,1)S(1)}, bf16[8,16,64]{2,1,0:T(8...) while((s32[]{:T(128)}, f32[8,16,128]{2,1,0:T(8,128)S(1)}, ...), condition=%wide.region_2.5_spmd, body=%wide.region_0.4_spmd.sunk | while | flops 17582176 | bytes 1926017 | solution.py:30
  87.2 3.2 %gather_fusion = bf16[1024,128]{1,0:T(8,128)(2,1)S(1)} fusion(bf16[128,2048]{0,1:T(8,128)(2,1)S(1)} %get-tuple-element.276, s32[1024]{0:T(1024)S(1)} %fusion.90), kind=kCustom, calls=%fused_computation.clone.clone.1 | custom fusion | bytes 528384 | tf_op jit(solution)/shard_map/while/body/eval_jaxpr/jit(_take)/gather | solution.py:17
  90.7 1.2 fusion.91
  92.7 3.2 %gather_fusion = bf16[1024,128]{1,0:T(8,128)(2,1)S(1)} fusion(bf16[128,2048]{0,1:T(8,128)(2,1)S(1)} %get-tuple-element.276, s32[1024]{0:T(1024)S(1)} %fusion.90), kind=kCustom, calls=%fused_computation.clone.clone.1 | custom fusion | bytes 528384 | tf_op jit(solution)/shard_map/while/body/eval_jaxpr/jit(_take)/gather | solution.py:17
  96.1 1.2 fusion.91
  98.1 3.2 %gather_fusion = bf16[1024,128]{1,0:T(8,128)(2,1)S(1)} fusion(bf16[128,2048]{0,1:T(8,128)(2,1)S(1)} %get-tuple-element.276, s32[1024]{0:T(1024)S(1)} %fusion.90), kind=kCustom, calls=%fused_computation.clone.clone.1 | custom fusion | bytes 528384 | tf_op jit(solution)/shard_map/while/body/eval_jaxpr/jit(_take)/gather | solution.py:17
  101.6 1.2 fusion.91
  103.6 3.2 %gather_fusion = bf16[1024,128]{1,0:T(8,128)(2,1)S(1)} fusion(bf16[128,2048]{0,1:T(8,128)(2,1)S(1)} %get-tuple-element.276, s32[1024]{0:T(1024)S(1)} %fusion.90), kind=kCustom, calls=%fused_computation.clone.clone.1 | custom fusion | bytes 528384 | tf_op jit(solution)/shard_map/while/body/eval_jaxpr/jit(_take)/gather | solution.py:17
  107.0 1.2 fusion.91
  109.0 3.2 %gather_fusion = bf16[1024,128]{1,0:T(8,128)(2,1)S(1)} fusion(bf16[128,2048]{0,1:T(8,128)(2,1)S(1)} %get-tuple-element.276, s32[1024]{0:T(1024)S(1)} %fusion.90), kind=kCustom, calls=%fused_computation.clone.clone.1 | custom fusion | bytes 528384 | tf_op jit(solution)/shard_map/while/body/eval_jaxpr/jit(_take)/gather | solution.py:17
  112.5 1.2 fusion.91
  114.4 3.2 %gather_fusion = bf16[1024,128]{1,0:T(8,128)(2,1)S(1)} fusion(bf16[128,2048]{0,1:T(8,128)(2,1)S(1)} %get-tuple-element.276, s32[1024]{0:T(1024)S(1)} %fusion.90), kind=kCustom, calls=%fused_computation.clone.clone.1 | custom fusion | bytes 528384 | tf_op jit(solution)/shard_map/while/body/eval_jaxpr/jit(_take)/gather | solution.py:17
  117.9 1.2 fusion.91
  119.9 3.2 %gather_fusion = bf16[1024,128]{1,0:T(8,128)(2,1)S(1)} fusion(bf16[128,2048]{0,1:T(8,128)(2,1)S(1)} %get-tuple-element.276, s32[1024]{0:T(1024)S(1)} %fusion.90), kind=kCustom, calls=%fused_computation.clone.clone.1 | custom fusion | bytes 528384 | tf_op jit(solution)/shard_map/while/body/eval_jaxpr/jit(_take)/gather | solution.py:17
  123.3 1.2 fusion.91
  125.3 3.2 %gather_fusion = bf16[1024,128]{1,0:T(8,128)(2,1)S(1)} fusion(bf16[128,2048]{0,1:T(8,128)(2,1)S(1)} %get-tuple-element.276, s32[1024]{0:T(1024)S(1)} %fusion.90), kind=kCustom, calls=%fused_computation.clone.clone.1 | custom fusion | bytes 528384 | tf_op jit(solution)/shard_map/while/body/eval_jaxpr/jit(_take)/gather | solution.py:17
  128.8 1.2 fusion.91
  132.5 52.5 %all-reduce.6.cloned.1.call-done = (f32[64,128]{1,0:T(8,128)}, f32[64,128]{1,0:T(8,128)}) async-done(((f32[64,128]{1,0:T(8,128)}, f32[64,128]{1,0:T(8,128)}), (f32[64,128]{1,0:T(8,128)}, f32[64,128]{1,0:T(8,128)})) %all-reduce.6.cloned.1.call-update) | async-done | bytes 65552 | tf_op jit(solution)/shard_map/psum | solution.py:81
  185.1 0.9 fusion.30
  186.0 0.9 fusion.35
  186.9 19.4 %all-reduce.3 = (f32[17,17]{0,1:T(8,128)S(1)}, f32[17,8]{1,0:T(8,128)S(1)}, f32[17,17]{0,1:T(8,128)S(1)}, f32[17,8]{1,0:T(8,128)S(1)}) all-reduce(f32[17,17]{0,1:T(8,128)S(1)} %fusion.32, f32[17,8]{1,0:T(8,128)S(1)} %fusion.30, f32[17,17]{0,1:T(8,128)S(1)} %fusion.37, ...), channel_id=1, replica_groups=mesh['set'=8,'path'=4] {'path'}, use_global_device_ids=true, to_apply=%region_12.18 | all-reduce | flops 850 | bytes 6800 | tf_op jit(solution)/shard_map/psum | solution.py:85
  206.5 1.5 cholesky.55
  209.4 1.3 custom-call.13
  212.1 1.5 cholesky.44
  215.0 1.3 custom-call.11
  (215 shorter events, 25.6 us)
Async XLA Ops:
  7.2 4.8 %copy-start.3 = (bf16[2,16,2048]{2,1,0:T(8,128)(2,1)S(1)}, bf16[2,16,2048]{2,1,0:T(8,128)(2,1)}, u32[]{:S(2)}) copy-start(bf16[2,16,2048]{2,1,0:T(8,128)(2,1)} %param.23) | copy-start | bytes 393220
  7.2 4.8 %copy-start.4 = (f32[2048]{0:T(1024)S(1)}, f32[2048]{0:T(1024)}, u32[]{:S(2)}) copy-start(f32[2048]{0:T(1024)} %param.25) | copy-start | bytes 24580
  7.2 34.2 %all-gather.2.cloned.1.call-start = ((), (), s32[]{:S(2)}) async-start(), calls=%async_computation | async-start | bytes 1179648 | tf_op jit(solution)/shard_map/all_gather | solution.py:75
  7.2 5.9 %copy-start = (bf16[2048,2048]{1,0:T(8,128)(2,1)S(1)}, bf16[2048,2048]{1,0:T(8,128)(2,1)}, u32[]{:S(2)}) copy-start(bf16[2048,2048]{1,0:T(8,128)(2,1)} %param.24) | copy-start | bytes 25165828
  13.1 2.0 copy-start.5
  13.1 2.1 copy-start.6
  13.1 2.2 copy-start.1
  13.1 6.7 %copy-start.8 = (s32[128]{0:T(128)S(1)}, s32[128]{0:T(128)}, u32[]{:S(2)}) copy-start(s32[128]{0:T(128)} %param.29) | copy-start | bytes 1540
  14.3 29.2 %copy-start.2 = (f32[16,2048]{1,0:T(8,128)}, f32[16,2048]{1,0:T(8,128)S(1)}, u32[]{:S(2)}) copy-start(f32[16,2048]{1,0:T(8,128)S(1)} %convolution_add_fusion) | copy-start | bytes 393220
  15.0 170.0 %all-reduce.6.cloned.1.call-start = ((), (), s32[]{:S(2)}) async-start(), calls=%async_computation.1 | async-start | bytes 131072 | tf_op jit(solution)/shard_map/psum | solution.py:81
  87.1 43.6 %copy-start.7 = (s32[128]{0:T(128)S(1)}, s32[128]{0:T(128)}, u32[]{:S(2)}) copy-start(s32[128]{0:T(128)} %param.30) | copy-start | bytes 1540
Sparse Core Ops, SparseCore 0:
  15.2 26.1 all-gather.1
  132.4 52.6 all-reduce.5
where the time goes:
time: 226 us; the launch traced here: 225 us
  waiting for transfers between devices  74.1 us (33%)
  local copies, waits for them, and re-layouts  69.6 us (31%)
  matrix products  31.6 us (14%)
  blocking collectives  19.4 us (9%)
  other arithmetic  15.1 us (7%)
  between operations  14.2 us (6%)
    psum x1, waiting for transfers between devices, per_device(): summed = lax.psum(jnp.dot(onehot, values, precision=high), 'set')  52.5 us
    gather x16, local copies, waits for them, and re-layouts, value_block(): jnp.take(slab, lists_b.reshape(-1), axis=1)  51.3 us
    all_gather x1, waiting for transfers between devices, per_device(): lax.all_gather(jnp.stack(slabs), 'set', axis=1, tiled=True)  21.5 us
    psum x1, blocking collectives, per_device(): lax.psum((jnp.dot(basis, basis.T, precision=high), jnp.dot(basis, netted....  19.4 us
    dot_general x16, matrix products, value_block(): jnp.einsum('psk,skl->psl', picked, gamma_b, preferred_element_type=jnp.fl...  19.2 us
    gather x16, local copies, waits for them, and re-layouts, value_block(): rates = jnp.exp(0.2 * jnp.take(slab, cur_b, axis=1).astype(jnp.float32))  9.2 us
    dot_general x2, matrix products, per_device(): jnp.dot(shocks[step], loading, preferred_element_type=jnp.float32)  5.93 us
    unnamed x21, local copies, waits for them, and re-layouts  5.85 us
  transfers between devices with their start and end apart: 2, of which 2 were waited for; matrix products, arithmetic and copies ran while one was open for 2% of the time, Pallas kernels for 0%

commit v1 on v0

v1 whole, which is shorter than its diff:
```python
import functools

import jax
import jax.numpy as jnp
from jax import lax
from jax.experimental import pallas as pl
from jax.experimental.pallas import tpu as pltpu
from jax.sharding import PartitionSpec as P

NB = 16
STEPS = 2
CP_DEV = 8
LANES = 128
CHUNK = 512
GROUP = 8
MESH = pl.DeviceIdType.MESH
HIGH = lax.Precision.HIGHEST
CONTRACT_LANES = (((1,), (1,)), ((), ()))


def sweep_inverse(a, size):
    rows = lax.broadcasted_iota(jnp.int32, a.shape, 0)
    cols = lax.broadcasted_iota(jnp.int32, a.shape, 1)
    for k in range(size):
        row = a[k : k + 1, :]
        col = a[:, k : k + 1]
        inv = 1.0 / a[k : k + 1, k : k + 1]
        scaled = row * inv
        update = a - col * scaled
        update = jnp.where(cols == k, col * inv, update)
        update = jnp.where(rows == k, jnp.where(cols == k, -inv, scaled), update)
        a = update
    return -a


def kernel(
    groups, zs, total_paths,
    start_hbm, shocks_hbm, loading_hbm, decay_ref, lists_hbm, delta_ref, gamma_hbm, cur_hbm, owner_ref,
    expo_ref, end_hbm,
    start_v, shocks_v, load_v, lists_s, cur_s, gin_v, end_v,
    gath, slab_t, gam, dlin, rates, xg, vals, basis, parts, rs, gsend, grecv, msend, mrecv,
    load_sem, misc_sem, slab_send, slab_fwd, slab_recv, rs_send, rs_recv, g_send, g_recv, m_send, m_recv,
):
    paths_dev = start_v.shape[0]
    factors = start_v.shape[1]
    depth, sets = lists_s.shape
    group_paths = paths_dev * groups
    pblocks = group_paths // LANES
    cc = STEPS * pblocks
    chunks = factors // CHUNK
    half = depth // 2
    cps = CP_DEV * groups
    width = NB + 1

    me = lax.axis_index("set")
    mz = lax.axis_index("path")
    sibling = me + 1 - 2 * lax.rem(me, 2)

    c_shocks = pltpu.make_async_copy(shocks_hbm, shocks_v, misc_sem.at[0])
    c_start = pltpu.make_async_copy(start_hbm, start_v, misc_sem.at[1])
    c_shocks.start()
    c_start.start()
    c_load = []
    for c in range(chunks):
        cols = pl.ds(c * CHUNK, CHUNK)
        cp = pltpu.make_async_copy(loading_hbm.at[:, cols], load_v.at[:, cols], load_sem.at[c])
        cp.start()
        c_load.append(cp)
    c_gamma = pltpu.make_async_copy(gamma_hbm, gin_v, misc_sem.at[2])
    c_lists = pltpu.make_async_copy(lists_hbm, lists_s, misc_sem.at[3])
    c_cur = pltpu.make_async_copy(cur_hbm, cur_s, misc_sem.at[4])
    c_gamma.start()
    c_lists.start()
    c_cur.start()

    barrier = pltpu.get_barrier_semaphore()
    for i in range(1, groups):
        pl.semaphore_signal(barrier, inc=1, device_id={"set": lax.rem(me + i, groups)}, device_id_type=MESH)
    for i in range(1, zs):
        pl.semaphore_signal(barrier, inc=1, device_id={"path": lax.rem(mz + i, zs)}, device_id_type=MESH)

    def slab_copy(owner, c, send, to):
        spot = gath.at[owner, :, pl.ds(c * CHUNK, CHUNK)]
        return pltpu.make_async_remote_copy(
            src_ref=spot, dst_ref=spot, send_sem=send, recv_sem=slab_recv.at[owner, c],
            device_id={"set": to}, device_id_type=MESH)

    sends = []
    c_shocks.wait()
    c_start.wait()
    for c in range(chunks):
        cols = pl.ds(c * CHUNK, CHUNK)
        c_load[c].wait()
        moved = jnp.dot(shocks_v[...], load_v[:, cols], preferred_element_type=jnp.float32)
        decay = decay_ref[:, cols]
        first = decay * start_v[:, cols] + moved[:paths_dev]
        second = decay * first + moved[paths_dev:]
        end_v[:, cols] = second
        gath[me, :paths_dev, cols] = first.astype(jnp.bfloat16)
        gath[me, paths_dev:, cols] = second.astype(jnp.bfloat16)
        if c == 0:
            pl.semaphore_wait(barrier, groups - 1 + zs - 1)
        for i in range(1, groups // 2):
            cp = slab_copy(me, c, slab_send.at[i, c], lax.rem(me + 2 * i, groups))
            cp.start()
            sends.append(cp)
        cp = slab_copy(me, c, slab_send.at[0, c], sibling)
        cp.start()
        sends.append(cp)
    c_end = pltpu.make_async_copy(end_v, end_hbm, misc_sem.at[5])
    c_end.start()

    c_gamma.wait()

    def relay(m, carry):
        upper = gin_v[pl.ds(pl.multiple_of(m * depth, depth), depth), :]
        lower = gin_v[pl.ds(pl.multiple_of((m + half) * depth, depth), depth), :]
        both = jnp.concatenate([upper, lower], axis=0).astype(jnp.float32)
        gam[pl.ds(m, sets, stride=half), :] = both.T
        return carry

    lax.fori_loop(0, half, relay, 0, unroll=4)
    dlin[...] = delta_ref[...].astype(jnp.float32).T

    def forward(c):
        for i in range(1, groups // 2):
            src = lax.rem(me + 2 * i, groups)
            slab_copy(src, c, slab_fwd.at[i, c], sibling).wait_recv()
            cp = slab_copy(src, c, slab_fwd.at[i, c], sibling)
            cp.start()
            sends.append(cp)

    def turn(c):
        slab_copy(sibling, c, slab_send.at[0, c], sibling).wait_recv()
        for i in range(1, groups // 2):
            slab_copy(lax.rem(sibling + 2 * i, groups), c, slab_fwd.at[i, c], sibling).wait_recv()
        for step in range(STEPS):
            for b in range(CHUNK // LANES):
                f0 = c * CHUNK + b * LANES
                block = gath[:, step * paths_dev : (step + 1) * paths_dev, f0 : f0 + LANES]
                block = block.reshape(group_paths, LANES).astype(jnp.float32).T
                for q in range(pblocks):
                    slab_t[pl.ds(f0 * cc + step * pblocks + q, LANES, stride=cc), :] = block[
                        :, q * LANES : (q + 1) * LANES
                    ]

    for c in range(chunks):
        forward(c)
        if c > 0:
            turn(c - 1)
    turn(chunks - 1)

    rates[...] = jnp.exp(0.2 * slab_t[: NB * cc, :])
    basis[...] = jnp.zeros_like(basis)
    for step in range(STEPS):
        for q in range(pblocks):
            basis[step, :NB, q * LANES : (q + 1) * LANES] = slab_t[pl.ds(step * pblocks + q, NB, stride=cc), :]
        basis[step, NB : NB + 1, :] = jnp.ones((1, group_paths), jnp.float32)
        gsend[step] = lax.dot_general(
            basis[step, : NB + 8, :], basis[step], CONTRACT_LANES, precision=HIGH,
            preferred_element_type=jnp.float32)
    for i in range(1, zs):
        cp = pltpu.make_async_remote_copy(
            src_ref=gsend, dst_ref=grecv.at[i], send_sem=g_send.at[i], recv_sem=g_recv.at[i],
            device_id={"path": lax.rem(mz + i, zs)}, device_id_type=MESH)
        cp.start()
        sends.append(cp)

    c_lists.wait()
    c_cur.wait()

    def revalue(g, carry):
        for u in range(GROUP):
            j = g * GROUP + u
            for k in range(depth):
                at = lists_s[k, j] * cc
                xg[u, k * cc : (k + 1) * cc, :] = slab_t[pl.ds(at, cc), :]
        rows = []
        for u in range(GROUP):
            j = g * GROUP + u
            x = jnp.concatenate([xg[u, pl.ds(c, depth, stride=cc), :] for c in range(cc)], axis=1)
            pair = gam[pl.ds(pl.multiple_of(j * half, half), half), :]
            linear = jnp.broadcast_to(dlin[pl.ds(j, 1), :], (16, depth))
            left = jnp.concatenate([pair[:, :depth], pair[:, depth:], linear], axis=0)
            prod = jnp.dot(left.astype(jnp.bfloat16), x.astype(jnp.bfloat16), preferred_element_type=jnp.float32)
            local = prod[depth : depth + 1] + 0.5 * jnp.sum(x * prod[:depth], axis=0, keepdims=True)
            at = cur_s[j] * cc
            rate = jnp.concatenate([rates[pl.ds(at + c, 1), :] for c in range(cc)], axis=1)
            rows.append(local * rate)
        vals[pl.ds(pl.multiple_of(g * GROUP, GROUP), GROUP), :] = jnp.concatenate(rows, axis=0)
        return carry

    lax.fori_loop(0, sets // GROUP, revalue, 0)

    owns = lax.broadcasted_iota(jnp.int32, (cps, sets), 0) == owner_ref[...]
    summed = jnp.dot(owns.astype(jnp.float32), vals[...], precision=HIGH, preferred_element_type=jnp.float32)
    parts[...] = summed.reshape(groups, CP_DEV, cc * LANES)
    for i in range(1, groups):
        to = lax.rem(me + i, groups)
        cp = pltpu.make_async_remote_copy(
            src_ref=parts.at[to], dst_ref=rs.at[i], send_sem=rs_send.at[i], recv_sem=rs_recv.at[i],
            device_id={"set": to}, device_id_type=MESH)
        cp.start()
        sends.append(cp)

    for i in range(1, zs):
        pltpu.make_async_remote_copy(
            src_ref=gsend, dst_ref=grecv.at[i], send_sem=g_send.at[i], recv_sem=g_recv.at[i],
            device_id={"path": lax.rem(mz + i, zs)}, device_id_type=MESH).wait_recv()
    eye = (lax.broadcasted_iota(jnp.int32, (NB + 8, LANES), 0) == lax.broadcasted_iota(jnp.int32, (NB + 8, LANES), 1))
    ridge = jnp.where(eye & (lax.broadcasted_iota(jnp.int32, (NB + 8, LANES), 0) < width), 0.001, 0.0)
    inverses = []
    for step in range(STEPS):
        gram = gsend[step]
        for i in range(1, zs):
            gram = gram + grecv[i, step]
        inverses.append(sweep_inverse(gram / total_paths + ridge, width))

    netted = parts[me]
    for i in range(1, groups):
        pltpu.make_async_remote_copy(
            src_ref=parts.at[0], dst_ref=rs.at[i], send_sem=rs_send.at[i], recv_sem=rs_recv.at[i],
            device_id={"set": lax.rem(me + i, groups)}, device_id_type=MESH).wait_recv()
        netted = netted + rs[i]
    for step in range(STEPS):
        msend[step] = lax.dot_general(
            netted[:, step * group_paths : (step + 1) * group_paths], basis[step], CONTRACT_LANES, precision=HIGH,
            preferred_element_type=jnp.float32)
    for i in range(1, zs):
        cp = pltpu.make_async_remote_copy(
            src_ref=msend, dst_ref=mrecv.at[i], send_sem=m_send.at[i], recv_sem=m_recv.at[i],
            device_id={"path": lax.rem(mz + i, zs)}, device_id_type=MESH)
        cp.start()
        sends.append(cp)
    for i in range(1, zs):
        pltpu.make_async_remote_copy(
            src_ref=msend, dst_ref=mrecv.at[i], send_sem=m_send.at[i], recv_sem=m_recv.at[i],
            device_id={"path": lax.rem(mz + i, zs)}, device_id_type=MESH).wait_recv()
    for step in range(STEPS):
        moments = msend[step]
        for i in range(1, zs):
            moments = moments + mrecv[i, step]
        moments = moments / total_paths
        coef = jnp.dot(moments[:, : NB + 8], inverses[step], precision=HIGH, preferred_element_type=jnp.float32)
        fitted = jnp.dot(
            coef[:, : NB + 8], basis[step, : NB + 8, :], precision=HIGH, preferred_element_type=jnp.float32)
        mine = netted[:, step * group_paths : (step + 1) * group_paths]
        expo_ref[step] = jnp.maximum(mine - 0.9 * fitted, 0.0)

    for cp in sends:
        cp.wait_send()
    c_end.wait()


def per_device(start_state, shocks, loading, decay, factor_lists, delta, gamma, currency, owner):
    groups = lax.axis_size("set")
    zs = lax.axis_size("path")
    paths_dev, factors = start_state.shape
    sets, depth = factor_lists.shape
    group_paths = paths_dev * groups
    cc = STEPS * group_paths // LANES
    chunks = factors // CHUNK
    any_spec = pl.BlockSpec(memory_space=pl.ANY)
    vmem = pl.BlockSpec(memory_space=pltpu.VMEM)
    f32, bf16 = jnp.float32, jnp.bfloat16
    dma = pltpu.SemaphoreType.DMA
    return pl.pallas_call(
        functools.partial(kernel, groups, zs, paths_dev * groups * zs),
        out_shape=(
            jax.ShapeDtypeStruct((STEPS, CP_DEV, group_paths), f32),
            jax.ShapeDtypeStruct((paths_dev, factors), f32),
        ),
        in_specs=[any_spec, any_spec, any_spec, vmem, any_spec, vmem, any_spec, any_spec, vmem],
        out_specs=(vmem, any_spec),
        scratch_shapes=[
            pltpu.VMEM((paths_dev, factors), f32),
            pltpu.VMEM((STEPS * paths_dev, factors), bf16),
            pltpu.VMEM((factors, factors), bf16),
            pltpu.SMEM((depth, sets), jnp.int32),
            pltpu.SMEM((sets,), jnp.int32),
            pltpu.VMEM((depth * depth, sets), bf16),
            pltpu.VMEM((paths_dev, factors), f32),
            pltpu.VMEM((groups, STEPS * paths_dev, factors), bf16),
            pltpu.VMEM((factors * cc, LANES), f32),
            pltpu.VMEM((sets * depth // 2, 2 * depth), f32),
            pltpu.VMEM((sets, depth), f32),
            pltpu.VMEM((NB * cc, LANES), f32),
            pltpu.VMEM((GROUP, depth * cc, LANES), f32),
            pltpu.VMEM((sets, cc * LANES), f32),
            pltpu.VMEM((STEPS, LANES, group_paths), f32),
            pltpu.VMEM((groups, CP_DEV, cc * LANES), f32),
            pltpu.VMEM((groups, CP_DEV, cc * LANES), f32),
            pltpu.VMEM((STEPS, NB + 8, LANES), f32),
            pltpu.VMEM((zs, STEPS, NB + 8, LANES), f32),
            pltpu.VMEM((STEPS, CP_DEV, LANES), f32),
            pltpu.VMEM((zs, STEPS, CP_DEV, LANES), f32),
            dma((chunks,)),
            dma((6,)),
            dma((groups, chunks)),
            dma((groups, chunks)),
            dma((groups, chunks)),
            dma((groups,)),
            dma((groups,)),
            dma((zs,)),
            dma((zs,)),
            dma((zs,)),
            dma((zs,)),
        ],
        compiler_params=pltpu.CompilerParams(
            collective_id=0, has_side_effects=True, vmem_limit_bytes=48 * 1024 * 1024
        ),
    )(
        start_state,
        shocks.reshape(STEPS * paths_dev, factors),
        loading,
        decay.reshape(1, factors),
        factor_lists.T,
        delta.T,
        jnp.transpose(gamma, (1, 2, 0)).reshape(depth * depth, sets),
        currency,
        owner.reshape(1, sets),
    )


def solution(mesh):
    return jax.shard_map(
        per_device,
        mesh=mesh,
        in_specs=(
            P(("path", "set"), None),
            P(None, ("path", "set"), None),
            P(),
            P(),
            P("set", None),
            P("set", None),
            P("set", None, None),
            P("set"),
            P("set"),
        ),
        out_specs=(P(None, "set", "path"), P(("path", "set"), None)),
        check_vma=False,
    )
```

time: 226 us -> 47.4 us (0.21)
  waiting for transfers between devices: 74.1 us -> 0 us
  local copies, waits for them, and re-layouts: 69.6 us -> 7.76 us
  Pallas kernels: 0 us -> 38.6 us
  matrix products: 31.6 us -> 0 us
  blocking collectives: 19.4 us -> 0 us
  other arithmetic: 15.1 us -> 0 us
  between operations: 14.2 us -> 0.66 us
    gather x32 -> x0, local copies, waits for them, and re-layouts: 60.5 us -> none  [the longest x16 51.3 us: value_block(): jnp.take(slab, lists_b.reshape(-1), axis=1)]
    psum x1 -> x0, waiting for transfers between devices: 52.5 us -> none  [per_device(): summed = lax.psum(jnp.dot(onehot, values, precision=high), 'set')]
    pallas_call x0 -> x1, Pallas kernels: none -> 38.6 us  [per_device(): pl.pallas_call(functools.partial(kernel, groups, zs, paths_dev * groups *...]
    dot_general x26 -> x0, matrix products: 30.9 us -> none  [the longest x16 19.2 us: value_block(): jnp.einsum('psk,skl->psl', picked, gamma_b, preferred_element_type=jnp.fl...]
    all_gather x1 -> x0, waiting for transfers between devices: 21.5 us -> none  [per_device(): lax.all_gather(jnp.stack(slabs), 'set', axis=1, tiled=True)]
    psum x1 -> x0, blocking collectives: 19.4 us -> none  [per_device(): lax.psum((jnp.dot(basis, basis.T, precision=high), jnp.dot(basis, netted....]
    another operation x13 -> x0, other arithmetic: 9.69 us -> none  [the longest x6 4.44 us: regress(): jnp.linalg.cholesky(gram / total + 0.001 * jnp.eye(size, dtype=jnp.float32))]
    select_n x16 -> x0, other arithmetic: 3.26 us -> none  [value_block(): jnp.take(slab, lists_b.reshape(-1), axis=1)]
  transfers between devices with their start and end apart: 2 -> 0, of which waited for: 2 -> 0; matrix products, arithmetic and copies ran while one was open for 2% -> 0% of each run, Pallas kernels for 0% -> 0%
where the time goes in v1:
time: 47.4 us; the launch traced here: 47.1 us
  Pallas kernels  38.6 us (81%)
  local copies, waits for them, and re-layouts  7.76 us (16%)
  between operations  0.66 us (1%)
    pallas_call x1, Pallas kernels, per_device(): pl.pallas_call(functools.partial(kernel, groups, zs, paths_dev * groups *...  38.6 us
    unnamed x18, local copies, waits for them, and re-layouts  7.76 us

profile of v1, /device:TPU:0, one launch (start us, length us, event | category | flops | bytes accessed | tf_op | source)
XLA Modules:
  0.0 47.1 jit_solution(13033064645767852265)
XLA Ops:
  0.6 0.0 copy-start
  0.6 1.2 %copy-done = bf16[128,64,64]{0,2,1:T(8,128)(2,1)S(1)} copy-done((bf16[128,64,64]{0,2,1:T(8,128)(2,1)S(1)}, bf16[128,64,64]{0,2,1:T(8,128)(2,1)}, u32[]{:S(2)}) %copy-start) | copy-done | bytes 1048600
  1.9 0.0 copy-start.1
  1.9 0.9 %copy-done.1 = f32[16,2048]{1,0:T(8,128)S(1)} copy-done((f32[16,2048]{1,0:T(8,128)S(1)}, f32[16,2048]{1,0:T(8,128)}, u32[]{:S(2)}) %copy-start.1) | copy-done | bytes 131096
  2.8 0.0 copy-start.2
  2.8 0.9 %copy-done.2 = bf16[2,16,2048]{2,1,0:T(8,128)(2,1)S(1)} copy-done((bf16[2,16,2048]{2,1,0:T(8,128)(2,1)S(1)}, bf16[2,16,2048]{2,1,0:T(8,128)(2,1)}, u32[]{:S(2)}) %copy-start.2) | copy-done | bytes 131096
  3.7 0.0 copy-start.3
  3.7 0.8 %copy-done.3 = s32[128,64]{0,1:T(8,128)S(1)} copy-done((s32[128,64]{0,1:T(8,128)S(1)}, s32[128,64]{0,1:T(8,128)}, u32[]{:S(2)}) %copy-start.3) | copy-done | bytes 32792
  4.4 0.0 copy-start.4
  4.4 0.7 %copy-done.4 = bf16[128,64]{0,1:T(8,128)(2,1)S(1)} copy-done((bf16[128,64]{0,1:T(8,128)(2,1)S(1)}, bf16[128,64]{0,1:T(8,128)(2,1)}, u32[]{:S(2)}) %copy-start.4) | copy-done | bytes 16408
  5.1 0.0 copy-start.5
  5.1 0.7 %copy-done.5 = f32[2048]{0:T(1024)S(1)} copy-done((f32[2048]{0:T(1024)S(1)}, f32[2048]{0:T(1024)}, u32[]{:S(2)}) %copy-start.5) | copy-done | bytes 8216
  5.8 0.0 copy-start.6
  5.8 0.7 %copy-done.6 = s32[128]{0:T(128)S(1)} copy-done((s32[128]{0:T(128)S(1)}, s32[128]{0:T(128)}, u32[]{:S(2)}) %copy-start.6) | copy-done | bytes 536
  6.5 0.0 copy-start.7
  6.5 0.7 %copy-done.7 = s32[128]{0:T(128)S(1)} copy-done((s32[128]{0:T(128)S(1)}, s32[128]{0:T(128)}, u32[]{:S(2)}) %copy-start.7) | copy-done | bytes 536
  7.2 38.6 %shard_map.104 = (f32[2,8,128]{2,1,0:T(8,128)S(1)}, f32[16,2048]{1,0:T(8,128)S(1)}) custom-call(f32[16,2048]{1,0:T(8,128)S(1)} %copy-done.1, bf16[32,2048]{1,0:T(8,128)(2,1)S(1)} %bitcast.9, bf16[2048,2048]{1,0:T(8,128)(2,1)} %loading_hbm.1, f32[1,2048]{1,0:T(1,128)S(1)} %bitcast.12, s32[64,128]{1,0:T(8,128)S(1)} %bitcast.10, bf16[64,128]{1,0:T(8,128)(2,1)S(1)} %bitcast.11, ...), custom_call_target="tpu_custom_call" | custom-call | tf_op jit(solution)/shard_map/pallas_call | solution.py:267
  45.8 0.6 %copy.13 = f32[2,8,128]{2,1,0:T(8,128)} copy(f32[2,8,128]{2,1,0:T(8,128)S(1)} %get-tuple-element.4) | data formatting | bytes 16384
  46.4 0.7 %copy.14 = f32[16,2048]{1,0:T(8,128)} copy(f32[16,2048]{1,0:T(8,128)S(1)} %get-tuple-element.5) | data formatting | bytes 262144
Async XLA Ops:
  0.6 1.2 %copy-start = (bf16[128,64,64]{0,2,1:T(8,128)(2,1)S(1)}, bf16[128,64,64]{0,2,1:T(8,128)(2,1)}, u32[]{:S(2)}) copy-start(bf16[128,64,64]{0,2,1:T(8,128)(2,1)} %param.15) | copy-start | bytes 3145732
  1.9 0.9 %copy-start.1 = (f32[16,2048]{1,0:T(8,128)S(1)}, f32[16,2048]{1,0:T(8,128)}, u32[]{:S(2)}) copy-start(f32[16,2048]{1,0:T(8,128)} %start_hbm.1) | copy-start | bytes 393220
  2.8 0.9 %copy-start.2 = (bf16[2,16,2048]{2,1,0:T(8,128)(2,1)S(1)}, bf16[2,16,2048]{2,1,0:T(8,128)(2,1)}, u32[]{:S(2)}) copy-start(bf16[2,16,2048]{2,1,0:T(8,128)(2,1)} %param.10) | copy-start | bytes 393220
  3.7 0.8 %copy-start.3 = (s32[128,64]{0,1:T(8,128)S(1)}, s32[128,64]{0,1:T(8,128)}, u32[]{:S(2)}) copy-start(s32[128,64]{0,1:T(8,128)} %param.13) | copy-start | bytes 98308
  4.4 0.7 %copy-start.4 = (bf16[128,64]{0,1:T(8,128)(2,1)S(1)}, bf16[128,64]{0,1:T(8,128)(2,1)}, u32[]{:S(2)}) copy-start(bf16[128,64]{0,1:T(8,128)(2,1)} %param.14) | copy-start | bytes 49156
  5.1 0.7 %copy-start.5 = (f32[2048]{0:T(1024)S(1)}, f32[2048]{0:T(1024)}, u32[]{:S(2)}) copy-start(f32[2048]{0:T(1024)} %param.12) | copy-start | bytes 24580
  5.8 0.7 %copy-start.6 = (s32[128]{0:T(128)S(1)}, s32[128]{0:T(128)}, u32[]{:S(2)}) copy-start(s32[128]{0:T(128)} %cur_hbm.1) | copy-start | bytes 1540
  6.5 0.7 %copy-start.7 = (s32[128]{0:T(128)S(1)}, s32[128]{0:T(128)}, u32[]{:S(2)}) copy-start(s32[128]{0:T(128)} %param.17) | copy-start | bytes 1540

commit v2 on v1

--- a/solution.py
+++ b/solution.py
@@ -12,6 +12,7 @@
 CP_DEV = 8
 LANES = 128
 CHUNK = 512
+PAD = 8
 GROUP = 8
 MESH = pl.DeviceIdType.MESH
 HIGH = lax.Precision.HIGHEST
@@ -35,10 +36,10 @@
 
 def kernel(
     groups, zs, total_paths,
-    start_hbm, shocks_hbm, loading_hbm, decay_ref, lists_hbm, delta_ref, gamma_hbm, cur_hbm, owner_ref,
-    expo_ref, end_hbm,
-    start_v, shocks_v, load_v, lists_s, cur_s, gin_v, end_v,
-    gath, slab_t, gam, dlin, rates, xg, vals, basis, parts, rs, gsend, grecv, msend, mrecv,
+    start_hbm, shocks_hbm, loading_hbm, decay_hbm, lists_hbm, delta_hbm, gamma_hbm, cur_hbm, owner_hbm,
+    expo_hbm, end_hbm,
+    start_v, shocks_v, load_v, decay_ref, lists_s, delta_ref, cur_s, owner_ref, gin_v, end_v, expo_ref,
+    gath, slab_t, gam, dlin, left, rates, xg, vals, basis, parts, rs, gsend, grecv, msend, mrecv,
     load_sem, misc_sem, slab_send, slab_fwd, slab_recv, rs_send, rs_recv, g_send, g_recv, m_send, m_recv,
 ):
     paths_dev = start_v.shape[0]
@@ -58,8 +59,10 @@
 
     c_shocks = pltpu.make_async_copy(shocks_hbm, shocks_v, misc_sem.at[0])
     c_start = pltpu.make_async_copy(start_hbm, start_v, misc_sem.at[1])
+    c_decay = pltpu.make_async_copy(decay_hbm, decay_ref, misc_sem.at[8])
     c_shocks.start()
     c_start.start()
+    c_decay.start()
     c_load = []
     for c in range(chunks):
         cols = pl.ds(c * CHUNK, CHUNK)
@@ -69,9 +72,13 @@
     c_gamma = pltpu.make_async_copy(gamma_hbm, gin_v, misc_sem.at[2])
     c_lists = pltpu.make_async_copy(lists_hbm, lists_s, misc_sem.at[3])
     c_cur = pltpu.make_async_copy(cur_hbm, cur_s, misc_sem.at[4])
+    c_delta = pltpu.make_async_copy(delta_hbm, delta_ref, misc_sem.at[6])
+    c_owner = pltpu.make_async_copy(owner_hbm, owner_ref, misc_sem.at[7])
     c_gamma.start()
+    c_delta.start()
     c_lists.start()
     c_cur.start()
+    c_owner.start()
 
     barrier = pltpu.get_barrier_semaphore()
     for i in range(1, groups):
@@ -88,6 +95,7 @@
     sends = []
     c_shocks.wait()
     c_start.wait()
+    c_decay.wait()
     for c in range(chunks):
         cols = pl.ds(c * CHUNK, CHUNK)
         c_load[c].wait()
@@ -120,7 +128,16 @@
         return carry
 
     lax.fori_loop(0, half, relay, 0, unroll=4)
+    c_delta.wait()
     dlin[...] = delta_ref[...].astype(jnp.float32).T
+
+    def prepare(j, carry):
+        pair = gam[pl.ds(pl.multiple_of(j * half, half), half), :]
+        linear = jnp.broadcast_to(dlin[pl.ds(j, 1), :], (16, depth))
+        left[j] = jnp.concatenate([pair[:, :depth], pair[:, depth:], linear], axis=0).astype(jnp.bfloat16)
+        return carry
+
+    lax.fori_loop(0, sets, prepare, 0, unroll=4)
 
     def forward(c):
         for i in range(1, groups // 2):
@@ -140,7 +157,7 @@
                 block = gath[:, step * paths_dev : (step + 1) * paths_dev, f0 : f0 + LANES]
                 block = block.reshape(group_paths, LANES).astype(jnp.float32).T
                 for q in range(pblocks):
-                    slab_t[pl.ds(f0 * cc + step * pblocks + q, LANES, stride=cc), :] = block[
+                    slab_t[pl.ds(PAD + f0 * cc + step * pblocks + q, LANES, stride=cc), :] = block[
                         :, q * LANES : (q + 1) * LANES
                     ]
 
@@ -150,11 +167,11 @@
             turn(c - 1)
     turn(chunks - 1)
 
-    rates[...] = jnp.exp(0.2 * slab_t[: NB * cc, :])
+    rates[...] = jnp.exp(0.2 * slab_t[PAD : PAD + NB * cc, :])
     basis[...] = jnp.zeros_like(basis)
     for step in range(STEPS):
         for q in range(pblocks):
-            basis[step, :NB, q * LANES : (q + 1) * LANES] = slab_t[pl.ds(step * pblocks + q, NB, stride=cc), :]
+            basis[step, :NB, q * LANES : (q + 1) * LANES] = slab_t[pl.ds(PAD + step * pblocks + q, NB, stride=cc), :]
         basis[step, NB : NB + 1, :] = jnp.ones((1, group_paths), jnp.float32)
         gsend[step] = lax.dot_general(
             basis[step, : NB + 8, :], basis[step], CONTRACT_LANES, precision=HIGH,
@@ -169,20 +186,24 @@
     c_lists.wait()
     c_cur.wait()
 
+    merged = max(1, PAD // cc)
+    span = merged * cc
+    sublane = lax.broadcasted_iota(jnp.int32, (span, LANES), 0)
+
     def revalue(g, carry):
         for u in range(GROUP):
             j = g * GROUP + u
-            for k in range(depth):
-                at = lists_s[k, j] * cc
-                xg[u, k * cc : (k + 1) * cc, :] = slab_t[pl.ds(at, cc), :]
+            for k in range(0, depth, merged):
+                rows = slab_t[pl.ds(lists_s[k, j] * cc + PAD, span), :]
+                for r in range(1, merged):
+                    window = slab_t[pl.ds(lists_s[k + r, j] * cc + (PAD - r * cc), span), :]
+                    rows = jnp.where(sublane >= r * cc, window, rows)
+                xg[u, k * cc : k * cc + span, :] = rows
         rows = []
         for u in range(GROUP):
             j = g * GROUP + u
             x = jnp.concatenate([xg[u, pl.ds(c, depth, stride=cc), :] for c in range(cc)], axis=1)
-            pair = gam[pl.ds(pl.multiple_of(j * half, half), half), :]
-            linear = jnp.broadcast_to(dlin[pl.ds(j, 1), :], (16, depth))
-            left = jnp.concatenate([pair[:, :depth], pair[:, depth:], linear], axis=0)
-            prod = jnp.dot(left.astype(jnp.bfloat16), x.astype(jnp.bfloat16), preferred_element_type=jnp.float32)
+            prod = jnp.dot(left[j], x.astype(jnp.bfloat16), preferred_element_type=jnp.float32)
             local = prod[depth : depth + 1] + 0.5 * jnp.sum(x * prod[:depth], axis=0, keepdims=True)
             at = cur_s[j] * cc
             rate = jnp.concatenate([rates[pl.ds(at + c, 1), :] for c in range(cc)], axis=1)
@@ -192,6 +213,7 @@
 
     lax.fori_loop(0, sets // GROUP, revalue, 0)
 
+    c_owner.wait()
     owns = lax.broadcasted_iota(jnp.int32, (cps, sets), 0) == owner_ref[...]
     summed = jnp.dot(owns.astype(jnp.float32), vals[...], precision=HIGH, preferred_element_type=jnp.float32)
     parts[...] = summed.reshape(groups, CP_DEV, cc * LANES)
@@ -247,8 +269,11 @@
         mine = netted[:, step * group_paths : (step + 1) * group_paths]
         expo_ref[step] = jnp.maximum(mine - 0.9 * fitted, 0.0)
 
+    c_expo = pltpu.make_async_copy(expo_ref, expo_hbm, misc_sem.at[9])
+    c_expo.start()
     for cp in sends:
         cp.wait_send()
+    c_expo.wait()
     c_end.wait()
 
 
@@ -260,8 +285,7 @@
     group_paths = paths_dev * groups
     cc = STEPS * group_paths // LANES
     chunks = factors // CHUNK
-    any_spec = pl.BlockSpec(memory_space=pl.ANY)
-    vmem = pl.BlockSpec(memory_space=pltpu.VMEM)
+    hbm = pl.BlockSpec(memory_space=pltpu.HBM)
     f32, bf16 = jnp.float32, jnp.bfloat16
     dma = pltpu.SemaphoreType.DMA
     return pl.pallas_call(
@@ -270,20 +294,25 @@
             jax.ShapeDtypeStruct((STEPS, CP_DEV, group_paths), f32),
             jax.ShapeDtypeStruct((paths_dev, factors), f32),
         ),
-        in_specs=[any_spec, any_spec, any_spec, vmem, any_spec, vmem, any_spec, any_spec, vmem],
-        out_specs=(vmem, any_spec),
+        in_specs=[hbm] * 9,
+        out_specs=(hbm, hbm),
         scratch_shapes=[
             pltpu.VMEM((paths_dev, factors), f32),
             pltpu.VMEM((STEPS * paths_dev, factors), bf16),
             pltpu.VMEM((factors, factors), bf16),
+            pltpu.VMEM((1, factors), f32),
             pltpu.SMEM((depth, sets), jnp.int32),
+            pltpu.VMEM((depth, sets), bf16),
             pltpu.SMEM((sets,), jnp.int32),
+            pltpu.VMEM((1, sets), jnp.int32),
             pltpu.VMEM((depth * depth, sets), bf16),
             pltpu.VMEM((paths_dev, factors), f32),
+            pltpu.VMEM((STEPS, CP_DEV, group_paths), f32),
             pltpu.VMEM((groups, STEPS * paths_dev, factors), bf16),
-            pltpu.VMEM((factors * cc, LANES), f32),
+            pltpu.VMEM((factors * cc + 2 * PAD, LANES), f32),
             pltpu.VMEM((sets * depth // 2, 2 * depth), f32),
             pltpu.VMEM((sets, depth), f32),
+            pltpu.VMEM((sets, depth + 16, depth), bf16),
             pltpu.VMEM((NB * cc, LANES), f32),
             pltpu.VMEM((GROUP, depth * cc, LANES), f32),
             pltpu.VMEM((sets, cc * LANES), f32),
@@ -295,7 +324,7 @@
             pltpu.VMEM((STEPS, CP_DEV, LANES), f32),
             pltpu.VMEM((zs, STEPS, CP_DEV, LANES), f32),
             dma((chunks,)),
-            dma((6,)),
+            dma((10,)),
             dma((groups, chunks)),
             dma((groups, chunks)),
             dma((groups, chunks)),
@@ -307,7 +336,7 @@
             dma((zs,)),
         ],
         compiler_params=pltpu.CompilerParams(
-            collective_id=0, has_side_effects=True, vmem_limit_bytes=48 * 1024 * 1024
+            collective_id=0, has_side_effects=True, vmem_limit_bytes=56 * 1024 * 1024
         ),
     )(
         start_state,

time: 47.4 us -> 43 us (0.907)
  local copies, waits for them, and re-layouts: 7.76 us -> 2.86 us
  Pallas kernels: 38.6 us -> 39.3 us
    unnamed x18 -> x2, local copies, waits for them, and re-layouts: 7.76 us -> 2.86 us
    pallas_call x1, Pallas kernels: 38.6 us -> 39.3 us  [per_device(): pl.pallas_call(functools.partial(kernel, groups, zs, paths_dev * groups *...]
where the time goes in v2:
time: 43 us; the launch traced here: 42.8 us
  Pallas kernels  39.3 us (91%)
  local copies, waits for them, and re-layouts  2.86 us (7%)
  between operations  0.64 us (1%)
    pallas_call x1, Pallas kernels, per_device(): pl.pallas_call(functools.partial(kernel, groups, zs, paths_dev * groups *...  39.3 us
    unnamed x2, local copies, waits for them, and re-layouts  2.86 us

profile of v2, /device:TPU:0, one launch (start us, length us, event | category | flops | bytes accessed | tf_op | source)
XLA Modules:
  0.0 42.8 jit_solution(4889947260129138507)
XLA Ops:
  0.6 39.3 %shard_map.104 = (f32[2,8,128]{2,1,0:T(8,128)}, f32[16,2048]{1,0:T(8,128)}) custom-call(f32[16,2048]{1,0:T(8,128)} %start_hbm.1, bf16[32,2048]{1,0:T(8,128)(2,1)} %bitcast.9, bf16[2048,2048]{1,0:T(8,128)(2,1)} %loading_hbm.1, f32[1,2048]{1,0:T(1,128)} %bitcast.12, s32[64,128]{1,0:T(8,128)} %bitcast.10, bf16[64,128]{1,0:T(8,128)(2,1)} %bitcast.11, ...), custom_call_target="tpu_custom_call" | custom-call | tf_op jit(solution)/shard_map/pallas_call | solution.py:291
  39.9 1.3 %copy.13 = f32[2,8,128]{2,1,0:T(8,128)} copy(f32[2,8,128]{2,1,0:T(8,128)} %get-tuple-element.4) | data formatting | bytes 16384
  41.2 1.6 %copy.14 = f32[16,2048]{1,0:T(8,128)} copy(f32[16,2048]{1,0:T(8,128)} %get-tuple-element.5) | data formatting | bytes 262144

commit v3 on v2

--- a/solution.py
+++ b/solution.py
@@ -37,8 +37,8 @@
 def kernel(
     groups, zs, total_paths,
     start_hbm, shocks_hbm, loading_hbm, decay_hbm, lists_hbm, delta_hbm, gamma_hbm, cur_hbm, owner_hbm,
-    expo_hbm, end_hbm,
-    start_v, shocks_v, load_v, decay_ref, lists_s, delta_ref, cur_s, owner_ref, gin_v, end_v, expo_ref,
+    expo_ref, end_v,
+    start_v, shocks_v, load_v, decay_ref, lists_s, delta_ref, cur_s, owner_ref, gin_v,
     gath, slab_t, gam, dlin, left, rates, xg, vals, basis, parts, rs, gsend, grecv, msend, mrecv,
     load_sem, misc_sem, slab_send, slab_fwd, slab_recv, rs_send, rs_recv, g_send, g_recv, m_send, m_recv,
 ):
@@ -115,10 +115,6 @@
         cp = slab_copy(me, c, slab_send.at[0, c], sibling)
         cp.start()
         sends.append(cp)
-    c_end = pltpu.make_async_copy(end_v, end_hbm, misc_sem.at[5])
-    c_end.start()
-
-    c_gamma.wait()
 
     def relay(m, carry):
         upper = gin_v[pl.ds(pl.multiple_of(m * depth, depth), depth), :]
@@ -127,17 +123,23 @@
         gam[pl.ds(m, sets, stride=half), :] = both.T
         return carry
 
-    lax.fori_loop(0, half, relay, 0, unroll=4)
-    c_delta.wait()
-    dlin[...] = delta_ref[...].astype(jnp.float32).T
-
     def prepare(j, carry):
         pair = gam[pl.ds(pl.multiple_of(j * half, half), half), :]
         linear = jnp.broadcast_to(dlin[pl.ds(j, 1), :], (16, depth))
         left[j] = jnp.concatenate([pair[:, :depth], pair[:, depth:], linear], axis=0).astype(jnp.bfloat16)
         return carry
 
-    lax.fori_loop(0, sets, prepare, 0, unroll=4)
+    def piece(c):
+        early = chunks // 2
+        if c == 0:
+            c_gamma.wait()
+            c_delta.wait()
+            dlin[...] = delta_ref[...].astype(jnp.float32).T
+        if c < early:
+            lax.fori_loop(half * c // early, half * (c + 1) // early, relay, 0, unroll=4)
+        else:
+            at, late = c - early, chunks - early
+            lax.fori_loop(sets * at // late, sets * (at + 1) // late, prepare, 0, unroll=8)
 
     def forward(c):
         for i in range(1, groups // 2):
@@ -161,27 +163,33 @@
                         :, q * LANES : (q + 1) * LANES
                     ]
 
+    def send_gram():
+        rates[...] = jnp.exp(0.2 * slab_t[PAD : PAD + NB * cc, :])
+        basis[...] = jnp.zeros_like(basis)
+        for step in range(STEPS):
+            for q in range(pblocks):
+                basis[step, :NB, q * LANES : (q + 1) * LANES] = slab_t[
+                    pl.ds(PAD + step * pblocks + q, NB, stride=cc), :
+                ]
+            basis[step, NB : NB + 1, :] = jnp.ones((1, group_paths), jnp.float32)
+            gsend[step] = lax.dot_general(
+                basis[step, : NB + 8, :], basis[step], CONTRACT_LANES, precision=HIGH,
+                preferred_element_type=jnp.float32)
+        for i in range(1, zs):
+            cp = pltpu.make_async_remote_copy(
+                src_ref=gsend, dst_ref=grecv.at[i], send_sem=g_send.at[i], recv_sem=g_recv.at[i],
+                device_id={"path": lax.rem(mz + i, zs)}, device_id_type=MESH)
+            cp.start()
+            sends.append(cp)
+
     for c in range(chunks):
+        piece(c)
         forward(c)
         if c > 0:
             turn(c - 1)
+        if c == 1:
+            send_gram()
     turn(chunks - 1)
-
-    rates[...] = jnp.exp(0.2 * slab_t[PAD : PAD + NB * cc, :])
-    basis[...] = jnp.zeros_like(basis)
-    for step in range(STEPS):
-        for q in range(pblocks):
-            basis[step, :NB, q * LANES : (q + 1) * LANES] = slab_t[pl.ds(PAD + step * pblocks + q, NB, stride=cc), :]
-        basis[step, NB : NB + 1, :] = jnp.ones((1, group_paths), jnp.float32)
-        gsend[step] = lax.dot_general(
-            basis[step, : NB + 8, :], basis[step], CONTRACT_LANES, precision=HIGH,
-            preferred_element_type=jnp.float32)
-    for i in range(1, zs):
-        cp = pltpu.make_async_remote_copy(
-            src_ref=gsend, dst_ref=grecv.at[i], send_sem=g_send.at[i], recv_sem=g_recv.at[i],
-            device_id={"path": lax.rem(mz + i, zs)}, device_id_type=MESH)
-        cp.start()
-        sends.append(cp)
 
     c_lists.wait()
     c_cur.wait()
@@ -190,32 +198,49 @@
     span = merged * cc
     sublane = lax.broadcasted_iota(jnp.int32, (span, LANES), 0)
 
-    def revalue(g, carry):
-        for u in range(GROUP):
-            j = g * GROUP + u
-            for k in range(0, depth, merged):
-                rows = slab_t[pl.ds(lists_s[k, j] * cc + PAD, span), :]
-                for r in range(1, merged):
-                    window = slab_t[pl.ds(lists_s[k + r, j] * cc + (PAD - r * cc), span), :]
-                    rows = jnp.where(sublane >= r * cc, window, rows)
-                xg[u, k * cc : k * cc + span, :] = rows
-        rows = []
-        for u in range(GROUP):
-            j = g * GROUP + u
-            x = jnp.concatenate([xg[u, pl.ds(c, depth, stride=cc), :] for c in range(cc)], axis=1)
-            prod = jnp.dot(left[j], x.astype(jnp.bfloat16), preferred_element_type=jnp.float32)
-            local = prod[depth : depth + 1] + 0.5 * jnp.sum(x * prod[:depth], axis=0, keepdims=True)
-            at = cur_s[j] * cc
-            rate = jnp.concatenate([rates[pl.ds(at + c, 1), :] for c in range(cc)], axis=1)
-            rows.append(local * rate)
-        vals[pl.ds(pl.multiple_of(g * GROUP, GROUP), GROUP), :] = jnp.concatenate(rows, axis=0)
+    def gather(buf, u, j):
+        for k in range(0, depth, merged):
+            rows = slab_t[pl.ds(lists_s[k, j] * cc + PAD, span), :]
+            for r in range(1, merged):
+                window = slab_t[pl.ds(lists_s[k + r, j] * cc + (PAD - r * cc), span), :]
+                rows = jnp.where(sublane >= r * cc, window, rows)
+            xg[buf, u, k * cc : k * cc + span, :] = rows
+
+    def value(buf, u, j):
+        x = jnp.concatenate([xg[buf, u, pl.ds(c, depth, stride=cc), :] for c in range(cc)], axis=1)
+        prod = jnp.dot(left[j], x.astype(jnp.bfloat16), preferred_element_type=jnp.float32)
+        local = prod[depth : depth + 1] + 0.5 * jnp.sum(x * prod[:depth], axis=0, keepdims=True)
+        at = cur_s[j] * cc
+        return local * jnp.concatenate([rates[pl.ds(at + c, 1), :] for c in range(cc)], axis=1)
+
+    rounds = sets // GROUP
+
+    def revalue(i, carry):
+        for buf in range(2):
+            g = 2 * i + buf
+            later = lax.rem(g + 1, rounds)
+            rows = []
+            for u in range(GROUP):
+                gather(1 - buf, u, later * GROUP + u)
+                rows.append(value(buf, u, g * GROUP + u))
+            vals[pl.ds(pl.multiple_of(g * GROUP, GROUP), GROUP), :] = jnp.concatenate(rows, axis=0)
         return carry
 
-    lax.fori_loop(0, sets // GROUP, revalue, 0)
+    for u in range(GROUP):
+        gather(0, u, u)
+    lax.fori_loop(0, rounds // 2, revalue, 0)
 
     c_owner.wait()
     owns = lax.broadcasted_iota(jnp.int32, (cps, sets), 0) == owner_ref[...]
-    summed = jnp.dot(owns.astype(jnp.float32), vals[...], precision=HIGH, preferred_element_type=jnp.float32)
+    owns = owns.astype(jnp.bfloat16)
+    value_f32 = vals[...]
+    high = value_f32.astype(jnp.bfloat16)
+    rest = value_f32 - high.astype(jnp.float32)
+    middle = rest.astype(jnp.bfloat16)
+    low = (rest - middle.astype(jnp.float32)).astype(jnp.bfloat16)
+    summed = jnp.dot(
+        jnp.concatenate([owns] * 3, axis=1), jnp.concatenate([high, middle, low], axis=0),
+        preferred_element_type=jnp.float32)
     parts[...] = summed.reshape(groups, CP_DEV, cc * LANES)
     for i in range(1, groups):
         to = lax.rem(me + i, groups)
@@ -231,12 +256,15 @@
             device_id={"path": lax.rem(mz + i, zs)}, device_id_type=MESH).wait_recv()
     eye = (lax.broadcasted_iota(jnp.int32, (NB + 8, LANES), 0) == lax.broadcasted_iota(jnp.int32, (NB + 8, LANES), 1))
     ridge = jnp.where(eye & (lax.broadcasted_iota(jnp.int32, (NB + 8, LANES), 0) < width), 0.001, 0.0)
-    inverses = []
+    fits = []
     for step in range(STEPS):
         gram = gsend[step]
         for i in range(1, zs):
             gram = gram + grecv[i, step]
-        inverses.append(sweep_inverse(gram / total_paths + ridge, width))
+        inverse = sweep_inverse(gram / total_paths + ridge, width)
+        fits.append(jnp.dot(
+            inverse[:, : NB + 8], basis[step, : NB + 8, :], precision=HIGH,
+            preferred_element_type=jnp.float32) / total_paths)
 
     netted = parts[me]
     for i in range(1, groups):
@@ -262,19 +290,12 @@
         moments = msend[step]
         for i in range(1, zs):
             moments = moments + mrecv[i, step]
-        moments = moments / total_paths
-        coef = jnp.dot(moments[:, : NB + 8], inverses[step], precision=HIGH, preferred_element_type=jnp.float32)
-        fitted = jnp.dot(
-            coef[:, : NB + 8], basis[step, : NB + 8, :], precision=HIGH, preferred_element_type=jnp.float32)
+        fitted = jnp.dot(moments[:, : NB + 8], fits[step], precision=HIGH, preferred_element_type=jnp.float32)
         mine = netted[:, step * group_paths : (step + 1) * group_paths]
         expo_ref[step] = jnp.maximum(mine - 0.9 * fitted, 0.0)
 
-    c_expo = pltpu.make_async_copy(expo_ref, expo_hbm, misc_sem.at[9])
-    c_expo.start()
     for cp in sends:
         cp.wait_send()
-    c_expo.wait()
-    c_end.wait()
 
 
 def per_device(start_state, shocks, loading, decay, factor_lists, delta, gamma, currency, owner):
@@ -286,6 +307,7 @@
     cc = STEPS * group_paths // LANES
     chunks = factors // CHUNK
     hbm = pl.BlockSpec(memory_space=pltpu.HBM)
+    vmem = pl.BlockSpec(memory_space=pltpu.VMEM)
     f32, bf16 = jnp.float32, jnp.bfloat16
     dma = pltpu.SemaphoreType.DMA
     return pl.pallas_call(
@@ -295,7 +317,7 @@
             jax.ShapeDtypeStruct((paths_dev, factors), f32),
         ),
         in_specs=[hbm] * 9,
-        out_specs=(hbm, hbm),
+        out_specs=(vmem, vmem),
         scratch_shapes=[
             pltpu.VMEM((paths_dev, factors), f32),
             pltpu.VMEM((STEPS * paths_dev, factors), bf16),
@@ -306,15 +328,13 @@
             pltpu.SMEM((sets,), jnp.int32),
             pltpu.VMEM((1, sets), jnp.int32),
             pltpu.VMEM((depth * depth, sets), bf16),
-            pltpu.VMEM((paths_dev, factors), f32),
-            pltpu.VMEM((STEPS, CP_DEV, group_paths), f32),
             pltpu.VMEM((groups, STEPS * paths_dev, factors), bf16),
             pltpu.VMEM((factors * cc + 2 * PAD, LANES), f32),
             pltpu.VMEM((sets * depth // 2, 2 * depth), f32),
             pltpu.VMEM((sets, depth), f32),
             pltpu.VMEM((sets, depth + 16, depth), bf16),
             pltpu.VMEM((NB * cc, LANES), f32),
-            pltpu.VMEM((GROUP, depth * cc, LANES), f32),
+            pltpu.VMEM((2, GROUP, depth * cc, LANES), f32),
             pltpu.VMEM((sets, cc * LANES), f32),
             pltpu.VMEM((STEPS, LANES, group_paths), f32),
             pltpu.VMEM((groups, CP_DEV, cc * LANES), f32),
@@ -336,7 +356,7 @@
             dma((zs,)),
         ],
         compiler_params=pltpu.CompilerParams(
-            collective_id=0, has_side_effects=True, vmem_limit_bytes=56 * 1024 * 1024
+            collective_id=0, has_side_effects=True, vmem_limit_bytes=40 * 1024 * 1024
         ),
     )(
         start_state,

time: 43 us -> 51.2 us (1.19)
  local copies, waits for them, and re-layouts: 2.86 us -> 11.1 us
    unnamed x2 -> x20, local copies, waits for them, and re-layouts: 2.86 us -> 11.1 us
where the time goes in v3:
time: 51.2 us; the launch traced here: 50.8 us
  Pallas kernels  39 us (76%)
  local copies, waits for them, and re-layouts  11.1 us (22%)
  between operations  0.66 us (1%)
    pallas_call x1, Pallas kernels, per_device(): pl.pallas_call(functools.partial(kernel, groups, zs, paths_dev * groups *...  39 us
    unnamed x20, local copies, waits for them, and re-layouts  11.1 us

profile of v3, /device:TPU:0, one launch (start us, length us, event | category | flops | bytes accessed | tf_op | source)
XLA Modules:
  0.0 50.8 jit_solution(16774393173832180729)
XLA Ops:
  0.6 0.0 copy-start
  0.6 3.4 %copy-done = bf16[2048,2048]{1,0:T(8,128)(2,1)S(1)} copy-done((bf16[2048,2048]{1,0:T(8,128)(2,1)S(1)}, bf16[2048,2048]{1,0:T(8,128)(2,1)}, u32[]{:S(2)}) %copy-start) | copy-done | bytes 8388632
  4.0 0.0 copy-start.1
  4.0 1.2 %copy-done.1 = bf16[128,64,64]{0,2,1:T(8,128)(2,1)S(1)} copy-done((bf16[128,64,64]{0,2,1:T(8,128)(2,1)S(1)}, bf16[128,64,64]{0,2,1:T(8,128)(2,1)}, u32[]{:S(2)}) %copy-start.1) | copy-done | bytes 1048600
  5.2 0.0 copy-start.2
  5.2 0.9 %copy-done.2 = f32[16,2048]{1,0:T(8,128)S(1)} copy-done((f32[16,2048]{1,0:T(8,128)S(1)}, f32[16,2048]{1,0:T(8,128)}, u32[]{:S(2)}) %copy-start.2) | copy-done | bytes 131096
  6.1 0.0 copy-start.3
  6.1 0.9 %copy-done.3 = bf16[2,16,2048]{2,1,0:T(8,128)(2,1)S(1)} copy-done((bf16[2,16,2048]{2,1,0:T(8,128)(2,1)S(1)}, bf16[2,16,2048]{2,1,0:T(8,128)(2,1)}, u32[]{:S(2)}) %copy-start.3) | copy-done | bytes 131096
  7.1 0.0 copy-start.4
  7.1 0.8 %copy-done.4 = s32[128,64]{0,1:T(8,128)S(1)} copy-done((s32[128,64]{0,1:T(8,128)S(1)}, s32[128,64]{0,1:T(8,128)}, u32[]{:S(2)}) %copy-start.4) | copy-done | bytes 32792
  7.8 0.0 copy-start.5
  7.8 0.7 %copy-done.5 = bf16[128,64]{0,1:T(8,128)(2,1)S(1)} copy-done((bf16[128,64]{0,1:T(8,128)(2,1)S(1)}, bf16[128,64]{0,1:T(8,128)(2,1)}, u32[]{:S(2)}) %copy-start.5) | copy-done | bytes 16408
  8.5 0.0 copy-start.6
  8.5 0.7 %copy-done.6 = f32[2048]{0:T(1024)S(1)} copy-done((f32[2048]{0:T(1024)S(1)}, f32[2048]{0:T(1024)}, u32[]{:S(2)}) %copy-start.6) | copy-done | bytes 8216
  9.2 0.0 copy-start.7
  9.2 0.7 %copy-done.7 = s32[128]{0:T(128)S(1)} copy-done((s32[128]{0:T(128)S(1)}, s32[128]{0:T(128)}, u32[]{:S(2)}) %copy-start.7) | copy-done | bytes 536
  9.9 0.0 copy-start.8
  9.9 0.7 %copy-done.8 = s32[128]{0:T(128)S(1)} copy-done((s32[128]{0:T(128)S(1)}, s32[128]{0:T(128)}, u32[]{:S(2)}) %copy-start.8) | copy-done | bytes 536
  10.5 39.0 %shard_map.104 = (f32[2,8,128]{2,1,0:T(8,128)S(1)}, f32[16,2048]{1,0:T(8,128)S(1)}) custom-call(f32[16,2048]{1,0:T(8,128)S(1)} %copy-done.2, bf16[32,2048]{1,0:T(8,128)(2,1)S(1)} %bitcast.9, bf16[2048,2048]{1,0:T(8,128)(2,1)S(1)} %copy-done, f32[1,2048]{1,0:T(1,128)S(1)} %bitcast.12, s32[64,128]{1,0:T(8,128)S(1)} %bitcast.10, bf16[64,128]{1,0:T(8,128)(2,1)S(1)} %bitcast.11, ...), custom_call_target="tpu_custom_call" | custom-call | tf_op jit(solution)/shard_map/pallas_call | solution.py:313
  49.5 0.6 %copy.13 = f32[2,8,128]{2,1,0:T(8,128)} copy(f32[2,8,128]{2,1,0:T(8,128)S(1)} %get-tuple-element.4) | data formatting | bytes 16384
  50.1 0.7 %copy.14 = f32[16,2048]{1,0:T(8,128)} copy(f32[16,2048]{1,0:T(8,128)S(1)} %get-tuple-element.5) | data formatting | bytes 262144
Async XLA Ops:
  0.6 3.4 %copy-start = (bf16[2048,2048]{1,0:T(8,128)(2,1)S(1)}, bf16[2048,2048]{1,0:T(8,128)(2,1)}, u32[]{:S(2)}) copy-start(bf16[2048,2048]{1,0:T(8,128)(2,1)} %loading_hbm.1) | copy-start | bytes 25165828
  4.0 1.2 %copy-start.1 = (bf16[128,64,64]{0,2,1:T(8,128)(2,1)S(1)}, bf16[128,64,64]{0,2,1:T(8,128)(2,1)}, u32[]{:S(2)}) copy-start(bf16[128,64,64]{0,2,1:T(8,128)(2,1)} %param.15) | copy-start | bytes 3145732
  5.2 0.9 %copy-start.2 = (f32[16,2048]{1,0:T(8,128)S(1)}, f32[16,2048]{1,0:T(8,128)}, u32[]{:S(2)}) copy-start(f32[16,2048]{1,0:T(8,128)} %start_hbm.1) | copy-start | bytes 393220
  6.1 0.9 %copy-start.3 = (bf16[2,16,2048]{2,1,0:T(8,128)(2,1)S(1)}, bf16[2,16,2048]{2,1,0:T(8,128)(2,1)}, u32[]{:S(2)}) copy-start(bf16[2,16,2048]{2,1,0:T(8,128)(2,1)} %param.10) | copy-start | bytes 393220
  7.1 0.8 %copy-start.4 = (s32[128,64]{0,1:T(8,128)S(1)}, s32[128,64]{0,1:T(8,128)}, u32[]{:S(2)}) copy-start(s32[128,64]{0,1:T(8,128)} %param.13) | copy-start | bytes 98308
  7.8 0.7 %copy-start.5 = (bf16[128,64]{0,1:T(8,128)(2,1)S(1)}, bf16[128,64]{0,1:T(8,128)(2,1)}, u32[]{:S(2)}) copy-start(bf16[128,64]{0,1:T(8,128)(2,1)} %param.14) | copy-start | bytes 49156
  8.5 0.7 %copy-start.6 = (f32[2048]{0:T(1024)S(1)}, f32[2048]{0:T(1024)}, u32[]{:S(2)}) copy-start(f32[2048]{0:T(1024)} %param.12) | copy-start | bytes 24580
  9.2 0.7 %copy-start.7 = (s32[128]{0:T(128)S(1)}, s32[128]{0:T(128)}, u32[]{:S(2)}) copy-start(s32[128]{0:T(128)} %cur_hbm.1) | copy-start | bytes 1540
  9.9 0.7 %copy-start.8 = (s32[128]{0:T(128)S(1)}, s32[128]{0:T(128)}, u32[]{:S(2)}) copy-start(s32[128]{0:T(128)} %param.17) | copy-start | bytes 1540

commit v4 on v3

--- a/solution.py
+++ b/solution.py
@@ -13,7 +13,7 @@
 LANES = 128
 CHUNK = 512
 PAD = 8
-GROUP = 8
+GROUP = 4
 MESH = pl.DeviceIdType.MESH
 HIGH = lax.Precision.HIGHEST
 CONTRACT_LANES = (((1,), (1,)), ((), ()))
@@ -37,8 +37,8 @@
 def kernel(
     groups, zs, total_paths,
     start_hbm, shocks_hbm, loading_hbm, decay_hbm, lists_hbm, delta_hbm, gamma_hbm, cur_hbm, owner_hbm,
-    expo_ref, end_v,
-    start_v, shocks_v, load_v, decay_ref, lists_s, delta_ref, cur_s, owner_ref, gin_v,
+    expo_hbm, end_hbm,
+    start_v, shocks_v, load_v, decay_ref, lists_s, delta_ref, cur_s, owner_ref, gin_v, end_v, expo_ref,
     gath, slab_t, gam, dlin, left, rates, xg, vals, basis, parts, rs, gsend, grecv, msend, mrecv,
     load_sem, misc_sem, slab_send, slab_fwd, slab_recv, rs_send, rs_recv, g_send, g_recv, m_send, m_recv,
 ):
@@ -50,6 +50,7 @@
     cc = STEPS * pblocks
     chunks = factors // CHUNK
     half = depth // 2
+    rounds = sets // GROUP
     cps = CP_DEV * groups
     width = NB + 1
 
@@ -63,12 +64,13 @@
     c_shocks.start()
     c_start.start()
     c_decay.start()
-    c_load = []
+
+    def load_copy(c):
+        cols = pl.ds(pl.multiple_of(c * CHUNK, CHUNK), CHUNK)
+        return pltpu.make_async_copy(loading_hbm.at[:, cols], load_v.at[:, cols], load_sem.at[c])
+
     for c in range(chunks):
-        cols = pl.ds(c * CHUNK, CHUNK)
-        cp = pltpu.make_async_copy(loading_hbm.at[:, cols], load_v.at[:, cols], load_sem.at[c])
-        cp.start()
-        c_load.append(cp)
+        load_copy(c).start()
     c_gamma = pltpu.make_async_copy(gamma_hbm, gin_v, misc_sem.at[2])
     c_lists = pltpu.make_async_copy(lists_hbm, lists_s, misc_sem.at[3])
     c_cur = pltpu.make_async_copy(cur_hbm, cur_s, misc_sem.at[4])
@@ -87,18 +89,22 @@
         pl.semaphore_signal(barrier, inc=1, device_id={"path": lax.rem(mz + i, zs)}, device_id_type=MESH)
 
     def slab_copy(owner, c, send, to):
-        spot = gath.at[owner, :, pl.ds(c * CHUNK, CHUNK)]
+        spot = gath.at[owner, :, pl.ds(pl.multiple_of(c * CHUNK, CHUNK), CHUNK)]
         return pltpu.make_async_remote_copy(
             src_ref=spot, dst_ref=spot, send_sem=send, recv_sem=slab_recv.at[owner, c],
             device_id={"set": to}, device_id_type=MESH)
+
+    left[...] = jnp.zeros_like(left)
 
     sends = []
     c_shocks.wait()
     c_start.wait()
     c_decay.wait()
-    for c in range(chunks):
-        cols = pl.ds(c * CHUNK, CHUNK)
-        c_load[c].wait()
+    pl.semaphore_wait(barrier, groups - 1 + zs - 1)
+
+    def evolve(c, carry):
+        cols = pl.ds(pl.multiple_of(c * CHUNK, CHUNK), CHUNK)
+        load_copy(c).wait()
         moved = jnp.dot(shocks_v[...], load_v[:, cols], preferred_element_type=jnp.float32)
         decay = decay_ref[:, cols]
         first = decay * start_v[:, cols] + moved[:paths_dev]
@@ -106,15 +112,14 @@
         end_v[:, cols] = second
         gath[me, :paths_dev, cols] = first.astype(jnp.bfloat16)
         gath[me, paths_dev:, cols] = second.astype(jnp.bfloat16)
-        if c == 0:
-            pl.semaphore_wait(barrier, groups - 1 + zs - 1)
         for i in range(1, groups // 2):
-            cp = slab_copy(me, c, slab_send.at[i, c], lax.rem(me + 2 * i, groups))
-            cp.start()
-            sends.append(cp)
-        cp = slab_copy(me, c, slab_send.at[0, c], sibling)
-        cp.start()
-        sends.append(cp)
+            slab_copy(me, c, slab_send.at[i, c], lax.rem(me + 2 * i, groups)).start()
+        slab_copy(me, c, slab_send.at[0, c], sibling).start()
+        return carry
+
+    lax.fori_loop(0, chunks, evolve, 0)
+    c_end = pltpu.make_async_copy(end_v, end_hbm, misc_sem.at[5])
+    c_end.start()
 
     def relay(m, carry):
         upper = gin_v[pl.ds(pl.multiple_of(m * depth, depth), depth), :]
@@ -123,10 +128,18 @@
         gam[pl.ds(m, sets, stride=half), :] = both.T
         return carry
 
-    def prepare(j, carry):
-        pair = gam[pl.ds(pl.multiple_of(j * half, half), half), :]
-        linear = jnp.broadcast_to(dlin[pl.ds(j, 1), :], (16, depth))
-        left[j] = jnp.concatenate([pair[:, :depth], pair[:, depth:], linear], axis=0).astype(jnp.bfloat16)
+    def prepare(q, carry):
+        for u in range(GROUP):
+            pair = gam[pl.ds(pl.multiple_of((q * GROUP + u) * half, half), half), :]
+            block = jnp.concatenate([pair[:, :depth], pair[:, depth:]], axis=0).astype(jnp.bfloat16)
+            left[q, u * depth : (u + 1) * depth, u * depth : (u + 1) * depth] = block
+        lines = []
+        for u in range(GROUP):
+            line = dlin[pl.ds(q * GROUP + u, 1), :]
+            none = jnp.zeros_like(line)
+            lines.append(jnp.concatenate([none] * u + [line] + [none] * (GROUP - 1 - u), axis=1))
+        lines.append(jnp.zeros((16 - GROUP, GROUP * depth), jnp.float32))
+        left[q, GROUP * depth :, :] = jnp.concatenate(lines, axis=0).astype(jnp.bfloat16)
         return carry
 
     def piece(c):
@@ -139,29 +152,31 @@
             lax.fori_loop(half * c // early, half * (c + 1) // early, relay, 0, unroll=4)
         else:
             at, late = c - early, chunks - early
-            lax.fori_loop(sets * at // late, sets * (at + 1) // late, prepare, 0, unroll=8)
+            lax.fori_loop(rounds * at // late, rounds * (at + 1) // late, prepare, 0, unroll=2)
 
     def forward(c):
         for i in range(1, groups // 2):
             src = lax.rem(me + 2 * i, groups)
             slab_copy(src, c, slab_fwd.at[i, c], sibling).wait_recv()
-            cp = slab_copy(src, c, slab_fwd.at[i, c], sibling)
-            cp.start()
-            sends.append(cp)
+            slab_copy(src, c, slab_fwd.at[i, c], sibling).start()
 
     def turn(c):
         slab_copy(sibling, c, slab_send.at[0, c], sibling).wait_recv()
         for i in range(1, groups // 2):
             slab_copy(lax.rem(sibling + 2 * i, groups), c, slab_fwd.at[i, c], sibling).wait_recv()
-        for step in range(STEPS):
-            for b in range(CHUNK // LANES):
-                f0 = c * CHUNK + b * LANES
-                block = gath[:, step * paths_dev : (step + 1) * paths_dev, f0 : f0 + LANES]
+
+        def flip(b, carry):
+            f0 = pl.multiple_of(c * CHUNK + b * LANES, LANES)
+            for step in range(STEPS):
+                block = gath[:, step * paths_dev : (step + 1) * paths_dev, pl.ds(f0, LANES)]
                 block = block.reshape(group_paths, LANES).astype(jnp.float32).T
                 for q in range(pblocks):
                     slab_t[pl.ds(PAD + f0 * cc + step * pblocks + q, LANES, stride=cc), :] = block[
                         :, q * LANES : (q + 1) * LANES
                     ]
+            return carry
+
+        lax.fori_loop(0, CHUNK // LANES, flip, 0, unroll=2)
 
     def send_gram():
         rates[...] = jnp.exp(0.2 * slab_t[PAD : PAD + NB * cc, :])
@@ -206,24 +221,33 @@
                 rows = jnp.where(sublane >= r * cc, window, rows)
             xg[buf, u, k * cc : k * cc + span, :] = rows
 
-    def value(buf, u, j):
-        x = jnp.concatenate([xg[buf, u, pl.ds(c, depth, stride=cc), :] for c in range(cc)], axis=1)
-        prod = jnp.dot(left[j], x.astype(jnp.bfloat16), preferred_element_type=jnp.float32)
-        local = prod[depth : depth + 1] + 0.5 * jnp.sum(x * prod[:depth], axis=0, keepdims=True)
-        at = cur_s[j] * cc
-        return local * jnp.concatenate([rates[pl.ds(at + c, 1), :] for c in range(cc)], axis=1)
-
-    rounds = sets // GROUP
+    def values(buf, g):
+        x = jnp.concatenate(
+            [
+                jnp.concatenate([xg[buf, u, pl.ds(c, depth, stride=cc), :] for c in range(cc)], axis=1)
+                for u in range(GROUP)
+            ],
+            axis=0,
+        )
+        prod = jnp.dot(left[g], x.astype(jnp.bfloat16), preferred_element_type=jnp.float32)
+        rows = []
+        for u in range(GROUP):
+            part = slice(u * depth, (u + 1) * depth)
+            linear = prod[GROUP * depth + u : GROUP * depth + u + 1]
+            local = linear + 0.5 * jnp.sum(x[part] * prod[part], axis=0, keepdims=True)
+            at = cur_s[g * GROUP + u] * cc
+            rows.append(local * jnp.concatenate([rates[pl.ds(at + c, 1), :] for c in range(cc)], axis=1))
+        return rows
 
     def revalue(i, carry):
+        rows = []
         for buf in range(2):
-            g = 2 * i + buf
-            later = lax.rem(g + 1, rounds)
-            rows = []
+            later = lax.rem(2 * i + buf + 1, rounds)
             for u in range(GROUP):
                 gather(1 - buf, u, later * GROUP + u)
-                rows.append(value(buf, u, g * GROUP + u))
-            vals[pl.ds(pl.multiple_of(g * GROUP, GROUP), GROUP), :] = jnp.concatenate(rows, axis=0)
+            rows += values(buf, 2 * i + buf)
+        both = 2 * GROUP
+        vals[pl.ds(pl.multiple_of(i * both, both), both), :] = jnp.concatenate(rows, axis=0)
         return carry
 
     for u in range(GROUP):
@@ -294,8 +318,30 @@
         mine = netted[:, step * group_paths : (step + 1) * group_paths]
         expo_ref[step] = jnp.maximum(mine - 0.9 * fitted, 0.0)
 
+    c_expo = pltpu.make_async_copy(expo_ref, expo_hbm, misc_sem.at[9])
+    c_expo.start()
+
+    def sent(c, carry):
+        slab_copy(me, c, slab_send.at[0, c], sibling).wait_send()
+        for i in range(1, groups // 2):
+            slab_copy(me, c, slab_send.at[i, c], sibling).wait_send()
+            slab_copy(me, c, slab_fwd.at[i, c], sibling).wait_send()
+        return carry
+
+    lax.fori_loop(0, chunks, sent, 0)
     for cp in sends:
         cp.wait_send()
+    c_expo.wait()
+    c_end.wait()
+
+
+def hand_on(expo_in, end_in, expo_out, end_out, sem):
+    first = pltpu.make_async_copy(expo_in, expo_out, sem.at[0])
+    second = pltpu.make_async_copy(end_in, end_out, sem.at[1])
+    first.start()
+    second.start()
+    first.wait()
+    second.wait()
 
 
 def per_device(start_state, shocks, loading, decay, factor_lists, delta, gamma, currency, owner):
@@ -307,17 +353,16 @@
     cc = STEPS * group_paths // LANES
     chunks = factors // CHUNK
     hbm = pl.BlockSpec(memory_space=pltpu.HBM)
-    vmem = pl.BlockSpec(memory_space=pltpu.VMEM)
     f32, bf16 = jnp.float32, jnp.bfloat16
     dma = pltpu.SemaphoreType.DMA
-    return pl.pallas_call(
+    results = pl.pallas_call(
         functools.partial(kernel, groups, zs, paths_dev * groups * zs),
         out_shape=(
             jax.ShapeDtypeStruct((STEPS, CP_DEV, group_paths), f32),
             jax.ShapeDtypeStruct((paths_dev, factors), f32),
         ),
         in_specs=[hbm] * 9,
-        out_specs=(vmem, vmem),
+        out_specs=(hbm, hbm),
         scratch_shapes=[
             pltpu.VMEM((paths_dev, factors), f32),
             pltpu.VMEM((STEPS * paths_dev, factors), bf16),
@@ -328,11 +373,13 @@
             pltpu.SMEM((sets,), jnp.int32),
             pltpu.VMEM((1, sets), jnp.int32),
             pltpu.VMEM((depth * depth, sets), bf16),
+            pltpu.VMEM((paths_dev, factors), f32),
+            pltpu.VMEM((STEPS, CP_DEV, group_paths), f32),
             pltpu.VMEM((groups, STEPS * paths_dev, factors), bf16),
             pltpu.VMEM((factors * cc + 2 * PAD, LANES), f32),
             pltpu.VMEM((sets * depth // 2, 2 * depth), f32),
             pltpu.VMEM((sets, depth), f32),
-            pltpu.VMEM((sets, depth + 16, depth), bf16),
+            pltpu.VMEM((sets // GROUP, GROUP * depth + 16, GROUP * depth), bf16),
             pltpu.VMEM((NB * cc, LANES), f32),
             pltpu.VMEM((2, GROUP, depth * cc, LANES), f32),
             pltpu.VMEM((sets, cc * LANES), f32),
@@ -356,7 +403,7 @@
             dma((zs,)),
         ],
         compiler_params=pltpu.CompilerParams(
-            collective_id=0, has_side_effects=True, vmem_limit_bytes=40 * 1024 * 1024
+            collective_id=0, has_side_effects=True, vmem_limit_bytes=60 * 1024 * 1024
         ),
     )(
         start_state,
@@ -369,6 +416,14 @@
         currency,
         owner.reshape(1, sets),
     )
+    return pl.pallas_call(
+        hand_on,
+        out_shape=tuple(jax.ShapeDtypeStruct(r.shape, r.dtype) for r in results),
+        in_specs=[hbm, hbm],
+        out_specs=(hbm, hbm),
+        scratch_shapes=[dma((2,))],
+        compiler_params=pltpu.CompilerParams(vmem_limit_bytes=60 * 1024 * 1024),
+    )(*results)
 
 
 def solution(mesh):

time: 51.2 us -> 47 us (0.918)
  local copies, waits for them, and re-layouts: 11.1 us -> 0 us
  Pallas kernels: 39 us -> 46.2 us
    unnamed x20 -> x0, local copies, waits for them, and re-layouts: 11.1 us -> none
    pallas_call x0 -> x1, Pallas kernels: none -> 5.34 us  [per_device(): pl.pallas_call(hand_on, out_shape=tuple((jax.ShapeDtypeStruct(r.shape, r....]
    pallas_call x1, Pallas kernels: 39 us -> 40.8 us  [per_device(): pl.pallas_call(functools.partial(kernel, groups, zs, paths_dev * groups *...]
where the time goes in v4:
time: 47 us; the launch traced here: 46.8 us
  Pallas kernels  46.2 us (98%)
  between operations  0.64 us (1%)
    pallas_call x1, Pallas kernels, per_device(): pl.pallas_call(functools.partial(kernel, groups, zs, paths_dev * groups *...  40.8 us
    pallas_call x1, Pallas kernels, per_device(): pl.pallas_call(hand_on, out_shape=tuple((jax.ShapeDtypeStruct(r.shape, r....  5.34 us

profile of v4, /device:TPU:0, one launch (start us, length us, event | category | flops | bytes accessed | tf_op | source)
XLA Modules:
  0.0 46.8 jit_solution(13668080202322564731)
XLA Ops:
  0.6 40.8 %shard_map.104 = (f32[2,8,128]{2,1,0:T(8,128)}, f32[16,2048]{1,0:T(8,128)}) custom-call(f32[16,2048]{1,0:T(8,128)} %start_hbm.1, bf16[32,2048]{1,0:T(8,128)(2,1)} %bitcast.9, bf16[2048,2048]{1,0:T(8,128)(2,1)} %loading_hbm.1, f32[1,2048]{1,0:T(1,128)} %bitcast.12, s32[64,128]{1,0:T(8,128)} %bitcast.10, bf16[64,128]{1,0:T(8,128)(2,1)} %bitcast.11, ...), custom_call_target="tpu_custom_call" | custom-call | tf_op jit(solution)/shard_map/pallas_call | solution.py:358
  41.5 5.3 %shard_map.105 = (f32[2,8,128]{2,1,0:T(8,128)}, f32[16,2048]{1,0:T(8,128)}) custom-call(f32[2,8,128]{2,1,0:T(8,128)} %get-tuple-element.4.expo_in, f32[16,2048]{1,0:T(8,128)} %get-tuple-element.5.end_in), custom_call_target="tpu_custom_call" | custom-call | tf_op jit(solution)/shard_map/pallas_call | solution.py:419

commit v5 on v3

--- a/solution.py
+++ b/solution.py
@@ -313,8 +313,8 @@
     return pl.pallas_call(
         functools.partial(kernel, groups, zs, paths_dev * groups * zs),
         out_shape=(
-            jax.ShapeDtypeStruct((STEPS, CP_DEV, group_paths), f32),
-            jax.ShapeDtypeStruct((paths_dev, factors), f32),
+            pltpu.VMEM((STEPS, CP_DEV, group_paths), f32),
+            pltpu.VMEM((paths_dev, factors), f32),
         ),
         in_specs=[hbm] * 9,
         out_specs=(vmem, vmem),
@@ -356,7 +356,7 @@
             dma((zs,)),
         ],
         compiler_params=pltpu.CompilerParams(
-            collective_id=0, has_side_effects=True, vmem_limit_bytes=40 * 1024 * 1024
+            collective_id=0, has_side_effects=True, vmem_limit_bytes=60 * 1024 * 1024
         ),
     )(
         start_state,

time: 51.2 us -> 39.9 us (0.78)
  local copies, waits for them, and re-layouts: 11.1 us -> 1.26 us
  Pallas kernels: 39 us -> 37.8 us
    unnamed x20 -> x2, local copies, waits for them, and re-layouts: 11.1 us -> 1.26 us
    pallas_call x1, Pallas kernels: 39 us -> 37.8 us  [per_device(): pl.pallas_call(functools.partial(kernel, groups, zs, paths_dev * groups *...]
where the time goes in v5:
time: 39.9 us; the launch traced here: 39.7 us
  Pallas kernels  37.8 us (95%)
  local copies, waits for them, and re-layouts  1.26 us (3%)
  between operations  0.64 us (2%)
    pallas_call x1, Pallas kernels, per_device(): pl.pallas_call(functools.partial(kernel, groups, zs, paths_dev * groups *...  37.8 us
    unnamed x2, local copies, waits for them, and re-layouts  1.26 us

profile of v5, /device:TPU:0, one launch (start us, length us, event | category | flops | bytes accessed | tf_op | source)
XLA Modules:
  0.0 39.7 jit_solution(2246978417310962502)
XLA Ops:
  0.6 37.8 %shard_map.104 = (f32[2,8,128]{2,1,0:T(8,128)S(1)}, f32[16,2048]{1,0:T(8,128)S(1)}) custom-call(f32[16,2048]{1,0:T(8,128)} %start_hbm.1, bf16[32,2048]{1,0:T(8,128)(2,1)} %bitcast.9, bf16[2048,2048]{1,0:T(8,128)(2,1)} %loading_hbm.1, f32[1,2048]{1,0:T(1,128)} %bitcast.12, s32[64,128]{1,0:T(8,128)} %bitcast.10, bf16[64,128]{1,0:T(8,128)(2,1)} %bitcast.11, ...), custom_call_target="tpu_custom_call" | custom-call | tf_op jit(solution)/shard_map/pallas_call | solution.py:313
  38.4 0.6 %copy.13 = f32[2,8,128]{2,1,0:T(8,128)} copy(f32[2,8,128]{2,1,0:T(8,128)S(1)} %get-tuple-element.2) | data formatting | bytes 16384
  39.0 0.7 %copy.14 = f32[16,2048]{1,0:T(8,128)} copy(f32[16,2048]{1,0:T(8,128)S(1)} %get-tuple-element.3) | data formatting | bytes 262144

commit v6 on v5

--- a/solution.py
+++ b/solution.py
@@ -39,7 +39,7 @@
     start_hbm, shocks_hbm, loading_hbm, decay_hbm, lists_hbm, delta_hbm, gamma_hbm, cur_hbm, owner_hbm,
     expo_ref, end_v,
     start_v, shocks_v, load_v, decay_ref, lists_s, delta_ref, cur_s, owner_ref, gin_v,
-    gath, slab_t, gam, dlin, left, rates, xg, vals, basis, parts, rs, gsend, grecv, msend, mrecv,
+    gath, slab_t, gam, dlin, left, rates, xg, vals, basis, parts, rs, gsend, grecv, bcat, hcat, mrecv,
     load_sem, misc_sem, slab_send, slab_fwd, slab_recv, rs_send, rs_recv, g_send, g_recv, m_send, m_recv,
 ):
     paths_dev = start_v.shape[0]
@@ -52,6 +52,7 @@
     half = depth // 2
     cps = CP_DEV * groups
     width = NB + 1
+    share = LANES // STEPS
 
     me = lax.axis_index("set")
     mz = lax.axis_index("path")
@@ -81,10 +82,13 @@
     c_owner.start()
 
     barrier = pltpu.get_barrier_semaphore()
-    for i in range(1, groups):
-        pl.semaphore_signal(barrier, inc=1, device_id={"set": lax.rem(me + i, groups)}, device_id_type=MESH)
-    for i in range(1, zs):
-        pl.semaphore_signal(barrier, inc=1, device_id={"path": lax.rem(mz + i, zs)}, device_id_type=MESH)
+    others = [(dz, ds) for dz in range(zs) for ds in range(groups) if dz or ds]
+
+    def place(dz, ds):
+        return {"path": lax.rem(mz + dz, zs), "set": lax.rem(me + ds, groups)}
+
+    for dz, ds in others:
+        pl.semaphore_signal(barrier, inc=1, device_id=place(dz, ds), device_id_type=MESH)
 
     def slab_copy(owner, c, send, to):
         spot = gath.at[owner, :, pl.ds(c * CHUNK, CHUNK)]
@@ -107,7 +111,7 @@
         gath[me, :paths_dev, cols] = first.astype(jnp.bfloat16)
         gath[me, paths_dev:, cols] = second.astype(jnp.bfloat16)
         if c == 0:
-            pl.semaphore_wait(barrier, groups - 1 + zs - 1)
+            pl.semaphore_wait(barrier, len(others))
         for i in range(1, groups // 2):
             cp = slab_copy(me, c, slab_send.at[i, c], lax.rem(me + 2 * i, groups))
             cp.start()
@@ -163,15 +167,21 @@
                         :, q * LANES : (q + 1) * LANES
                     ]
 
+    spots = [slice(step * share, step * share + NB + 8) for step in range(STEPS)]
+    spans = [slice(step * group_paths, (step + 1) * group_paths) for step in range(STEPS)]
+
     def send_gram():
         rates[...] = jnp.exp(0.2 * slab_t[PAD : PAD + NB * cc, :])
         basis[...] = jnp.zeros_like(basis)
+        bcat[...] = jnp.zeros_like(bcat)
+        hcat[...] = jnp.zeros_like(hcat)
         for step in range(STEPS):
             for q in range(pblocks):
                 basis[step, :NB, q * LANES : (q + 1) * LANES] = slab_t[
                     pl.ds(PAD + step * pblocks + q, NB, stride=cc), :
                 ]
             basis[step, NB : NB + 1, :] = jnp.ones((1, group_paths), jnp.float32)
+            bcat[spots[step], spans[step]] = basis[step, : NB + 8, :]
             gsend[step] = lax.dot_general(
                 basis[step, : NB + 8, :], basis[step], CONTRACT_LANES, precision=HIGH,
                 preferred_element_type=jnp.float32)
@@ -241,12 +251,23 @@
     summed = jnp.dot(
         jnp.concatenate([owns] * 3, axis=1), jnp.concatenate([high, middle, low], axis=0),
         preferred_element_type=jnp.float32)
-    parts[...] = summed.reshape(groups, CP_DEV, cc * LANES)
-    for i in range(1, groups):
-        to = lax.rem(me + i, groups)
-        cp = pltpu.make_async_remote_copy(
-            src_ref=parts.at[to], dst_ref=rs.at[i], send_sem=rs_send.at[i], recv_sem=rs_recv.at[i],
-            device_id={"set": to}, device_id_type=MESH)
+    parts[:, :, : cc * LANES] = summed.reshape(groups, CP_DEV, cc * LANES)
+    moments = lax.dot_general(summed, bcat[...], CONTRACT_LANES, precision=HIGH, preferred_element_type=jnp.float32)
+    parts[:, :, cc * LANES :] = moments.reshape(groups, CP_DEV, LANES)
+
+    def block_copy(dz, ds):
+        to = lax.rem(me + ds, groups)
+        if dz:
+            slot = dz * groups + ds
+            return pltpu.make_async_remote_copy(
+                src_ref=parts.at[to, :, pl.ds(cc * LANES, LANES)], dst_ref=mrecv.at[slot], send_sem=m_send.at[slot],
+                recv_sem=m_recv.at[slot], device_id=place(dz, ds), device_id_type=MESH)
+        return pltpu.make_async_remote_copy(
+            src_ref=parts.at[to], dst_ref=rs.at[ds], send_sem=rs_send.at[ds], recv_sem=rs_recv.at[ds],
+            device_id=place(dz, ds), device_id_type=MESH)
+
+    for dz, ds in others:
+        cp = block_copy(dz, ds)
         cp.start()
         sends.append(cp)
 
@@ -256,43 +277,29 @@
             device_id={"path": lax.rem(mz + i, zs)}, device_id_type=MESH).wait_recv()
     eye = (lax.broadcasted_iota(jnp.int32, (NB + 8, LANES), 0) == lax.broadcasted_iota(jnp.int32, (NB + 8, LANES), 1))
     ridge = jnp.where(eye & (lax.broadcasted_iota(jnp.int32, (NB + 8, LANES), 0) < width), 0.001, 0.0)
-    fits = []
     for step in range(STEPS):
         gram = gsend[step]
         for i in range(1, zs):
             gram = gram + grecv[i, step]
         inverse = sweep_inverse(gram / total_paths + ridge, width)
-        fits.append(jnp.dot(
+        hcat[spots[step], spans[step]] = jnp.dot(
             inverse[:, : NB + 8], basis[step, : NB + 8, :], precision=HIGH,
-            preferred_element_type=jnp.float32) / total_paths)
-
-    netted = parts[me]
-    for i in range(1, groups):
-        pltpu.make_async_remote_copy(
-            src_ref=parts.at[0], dst_ref=rs.at[i], send_sem=rs_send.at[i], recv_sem=rs_recv.at[i],
-            device_id={"set": lax.rem(me + i, groups)}, device_id_type=MESH).wait_recv()
-        netted = netted + rs[i]
+            preferred_element_type=jnp.float32) / total_paths
+
+    total = parts[me]
+    for dz, ds in others:
+        block_copy(dz, ds).wait_recv()
+        if not dz:
+            total = total + rs[ds]
+    netted = total[:, : cc * LANES]
+    moments = total[:, cc * LANES :]
+    for dz, ds in others:
+        if dz:
+            moments = moments + mrecv[dz * groups + ds]
+    fitted = jnp.dot(moments, hcat[...], precision=HIGH, preferred_element_type=jnp.float32)
+    result = jnp.maximum(netted - 0.9 * fitted, 0.0)
     for step in range(STEPS):
-        msend[step] = lax.dot_general(
-            netted[:, step * group_paths : (step + 1) * group_paths], basis[step], CONTRACT_LANES, precision=HIGH,
-            preferred_element_type=jnp.float32)
-    for i in range(1, zs):
-        cp = pltpu.make_async_remote_copy(
-            src_ref=msend, dst_ref=mrecv.at[i], send_sem=m_send.at[i], recv_sem=m_recv.at[i],
-            device_id={"path": lax.rem(mz + i, zs)}, device_id_type=MESH)
-        cp.start()
-        sends.append(cp)
-    for i in range(1, zs):
-        pltpu.make_async_remote_copy(
-            src_ref=msend, dst_ref=mrecv.at[i], send_sem=m_send.at[i], recv_sem=m_recv.at[i],
-            device_id={"path": lax.rem(mz + i, zs)}, device_id_type=MESH).wait_recv()
-    for step in range(STEPS):
-        moments = msend[step]
-        for i in range(1, zs):
-            moments = moments + mrecv[i, step]
-        fitted = jnp.dot(moments[:, : NB + 8], fits[step], precision=HIGH, preferred_element_type=jnp.float32)
-        mine = netted[:, step * group_paths : (step + 1) * group_paths]
-        expo_ref[step] = jnp.maximum(mine - 0.9 * fitted, 0.0)
+        expo_ref[step] = result[:, spans[step]]
 
     for cp in sends:
         cp.wait_send()
@@ -337,12 +344,13 @@
             pltpu.VMEM((2, GROUP, depth * cc, LANES), f32),
             pltpu.VMEM((sets, cc * LANES), f32),
             pltpu.VMEM((STEPS, LANES, group_paths), f32),
-            pltpu.VMEM((groups, CP_DEV, cc * LANES), f32),
-            pltpu.VMEM((groups, CP_DEV, cc * LANES), f32),
+            pltpu.VMEM((groups, CP_DEV, (cc + 1) * LANES), f32),
+            pltpu.VMEM((groups, CP_DEV, (cc + 1) * LANES), f32),
             pltpu.VMEM((STEPS, NB + 8, LANES), f32),
             pltpu.VMEM((zs, STEPS, NB + 8, LANES), f32),
-            pltpu.VMEM((STEPS, CP_DEV, LANES), f32),
-            pltpu.VMEM((zs, STEPS, CP_DEV, LANES), f32),
+            pltpu.VMEM((LANES, cc * LANES), f32),
+            pltpu.VMEM((LANES, cc * LANES), f32),
+            pltpu.VMEM((zs * groups, CP_DEV, LANES), f32),
             dma((chunks,)),
             dma((10,)),
             dma((groups, chunks)),
@@ -352,8 +360,8 @@
             dma((groups,)),
             dma((zs,)),
             dma((zs,)),
-            dma((zs,)),
-            dma((zs,)),
+            dma((zs * groups,)),
+            dma((zs * groups,)),
         ],
         compiler_params=pltpu.CompilerParams(
             collective_id=0, has_side_effects=True, vmem_limit_bytes=60 * 1024 * 1024

time: 39.9 us -> 38.3 us (0.960)
  Pallas kernels: 37.8 us -> 36.2 us
    pallas_call x1, Pallas kernels: 37.8 us -> 36.2 us  [per_device(): pl.pallas_call(functools.partial(kernel, groups, zs, paths_dev * groups *...]
where the time goes in v6:
time: 38.3 us; the launch traced here: 38.1 us
  Pallas kernels  36.2 us (95%)
  local copies, waits for them, and re-layouts  1.26 us (3%)
  between operations  0.64 us (2%)
    pallas_call x1, Pallas kernels, per_device(): pl.pallas_call(functools.partial(kernel, groups, zs, paths_dev * groups *...  36.2 us
    unnamed x2, local copies, waits for them, and re-layouts  1.26 us

profile of v6, /device:TPU:0, one launch (start us, length us, event | category | flops | bytes accessed | tf_op | source)
XLA Modules:
  0.0 38.1 jit_solution(6108903458857467695)
XLA Ops:
  0.6 36.2 %shard_map.104 = (f32[2,8,128]{2,1,0:T(8,128)S(1)}, f32[16,2048]{1,0:T(8,128)S(1)}) custom-call(f32[16,2048]{1,0:T(8,128)} %start_hbm.1, bf16[32,2048]{1,0:T(8,128)(2,1)} %bitcast.9, bf16[2048,2048]{1,0:T(8,128)(2,1)} %loading_hbm.1, f32[1,2048]{1,0:T(1,128)} %bitcast.12, s32[64,128]{1,0:T(8,128)} %bitcast.10, bf16[64,128]{1,0:T(8,128)(2,1)} %bitcast.11, ...), custom_call_target="tpu_custom_call" | custom-call | tf_op jit(solution)/shard_map/pallas_call | solution.py:320
  36.9 0.6 %copy.13 = f32[2,8,128]{2,1,0:T(8,128)} copy(f32[2,8,128]{2,1,0:T(8,128)S(1)} %get-tuple-element.2) | data formatting | bytes 16384
  37.5 0.7 %copy.14 = f32[16,2048]{1,0:T(8,128)} copy(f32[16,2048]{1,0:T(8,128)S(1)} %get-tuple-element.3) | data formatting | bytes 262144

commit v7 on v6

--- a/solution.py
+++ b/solution.py
@@ -11,7 +11,7 @@
 STEPS = 2
 CP_DEV = 8
 LANES = 128
-CHUNK = 512
+CHUNK = 256
 PAD = 8
 GROUP = 8
 MESH = pl.DeviceIdType.MESH

time: 38.3 us -> 39.8 us (1.039)
  Pallas kernels: 36.2 us -> 37.7 us
    pallas_call x1, Pallas kernels: 36.2 us -> 37.7 us  [per_device(): pl.pallas_call(functools.partial(kernel, groups, zs, paths_dev * groups *...]
where the time goes in v7:
time: 39.8 us; the launch traced here: 39.6 us
  Pallas kernels  37.7 us (95%)
  local copies, waits for them, and re-layouts  1.26 us (3%)
  between operations  0.64 us (2%)
    pallas_call x1, Pallas kernels, per_device(): pl.pallas_call(functools.partial(kernel, groups, zs, paths_dev * groups *...  37.7 us
    unnamed x2, local copies, waits for them, and re-layouts  1.26 us

profile of v7, /device:TPU:0, one launch (start us, length us, event | category | flops | bytes accessed | tf_op | source)
XLA Modules:
  0.0 39.6 jit_solution(4061928677029145764)
XLA Ops:
  0.6 37.7 %shard_map.104 = (f32[2,8,128]{2,1,0:T(8,128)S(1)}, f32[16,2048]{1,0:T(8,128)S(1)}) custom-call(f32[16,2048]{1,0:T(8,128)} %start_hbm.1, bf16[32,2048]{1,0:T(8,128)(2,1)} %bitcast.9, bf16[2048,2048]{1,0:T(8,128)(2,1)} %loading_hbm.1, f32[1,2048]{1,0:T(1,128)} %bitcast.12, s32[64,128]{1,0:T(8,128)} %bitcast.10, bf16[64,128]{1,0:T(8,128)(2,1)} %bitcast.11, ...), custom_call_target="tpu_custom_call" | custom-call | tf_op jit(solution)/shard_map/pallas_call | solution.py:320
  38.4 0.6 %copy.13 = f32[2,8,128]{2,1,0:T(8,128)} copy(f32[2,8,128]{2,1,0:T(8,128)S(1)} %get-tuple-element.2) | data formatting | bytes 16384
  39.0 0.7 %copy.14 = f32[16,2048]{1,0:T(8,128)} copy(f32[16,2048]{1,0:T(8,128)S(1)} %get-tuple-element.3) | data formatting | bytes 262144
